TPU v7x, 256 devices: a whole 4x4x8 slice. The times are simulated.
256 devices in a mesh: seq: 32 (over y, x, core), ch: 8 (over z).
Axes of the slice: x: 4, y: 4, z: 8, core: 2. Of those that a mesh axis runs over, the one named last changes fastest.
Arguments:
- gate_query: bfloat16 [16384, 4096], P('seq', 'ch'), may hold values from -6 to 6
- gate_key: bfloat16 [16384, 4096], P('seq', 'ch'), may hold values from -6 to 6
- gate_value: bfloat16 [16384, 4096], P('seq', 'ch'), may hold values from -6 to 6
- skip_gain: float32 [4096], P('ch'), may hold values from 0.5 to 1.5
- filter_spectra: bfloat16 [32768, 2, 4096], P('seq', None, 'ch'), may hold values from -9 to 9
- out_weight: bfloat16 [4096, 4096], P('ch'), may hold values from -0.09375 to 0.09375
Outputs:
- mixed: bfloat16 [16384, 4096], P('seq', 'ch')
All inputs are finite; a program needn't handle non-finite values.
Results may differ from a plain program's by a relative error of at most 0.0049.
Values may be sent and summed in bfloat16 or wider, within the bound.
A program may use at most 128 MiB of HBM per device.

v0:
```python
import math

import jax
import jax.numpy as jnp
from jax import lax
from jax.sharding import PartitionSpec as P

exact_mode = lax.Precision.HIGHEST


def phase_table(rows, cols, modulus, sign, row_start, col_start):
    row_index = lax.broadcasted_iota(jnp.int32, (rows, cols), 0) + row_start
    col_index = lax.broadcasted_iota(jnp.int32, (rows, cols), 1) + col_start
    wrapped = row_index * col_index % modulus
    theta = wrapped.astype(jnp.float32) * (sign * 2.0 * math.pi / modulus)
    return (jnp.cos(theta), jnp.sin(theta))


def contract(matrix, values):
    return jnp.einsum("ks,gsc->gkc", matrix, values, precision=exact_mode)


def transform(cos_mat, sin_mat, real_part, imag_part):
    out_real = contract(cos_mat, real_part) - contract(sin_mat, imag_part)
    out_imag = contract(cos_mat, imag_part) + contract(sin_mat, real_part)
    return (out_real, out_imag)


def complex_product(left_real, left_imag, right_real, right_imag):
    return (
        left_real * right_real - left_imag * right_imag,
        left_real * right_imag + left_imag * right_real,
    )


def body(gate_query, gate_key, gate_value, skip_gain, filter_spectra, out_weight):
    parts = lax.axis_size("seq")
    device_rank = lax.axis_index("seq")
    tokens = gate_key.shape[0]
    channels = gate_key.shape[1]
    stride = tokens // parts
    points = 2 * parts * tokens
    gated_in = gate_key.astype(jnp.float32) * gate_value.astype(jnp.float32)
    spread = lax.all_to_all(
        gated_in.reshape(parts, stride, channels), "seq", split_axis=0, concat_axis=0, tiled=True
    )
    cos_cross, sin_cross = phase_table(2 * parts, parts, 2 * parts, -1.0, 0, 0)
    flattened = spread.reshape(parts, stride * channels)
    upper_real = jnp.dot(cos_cross, flattened, precision=exact_mode).reshape(
        2 * parts, stride, channels
    )
    upper_imag = jnp.dot(sin_cross, flattened, precision=exact_mode).reshape(
        2 * parts, stride, channels
    )
    rot_cos, rot_sin = phase_table(2 * parts, stride, points, -1.0, 0, device_rank * stride)
    turned_real, turned_imag = complex_product(
        upper_real, upper_imag, rot_cos[:, :, None], rot_sin[:, :, None]
    )
    mid_real, mid_imag = (
        lax.all_to_all(turned_real, "seq", split_axis=0, concat_axis=1, tiled=True),
        lax.all_to_all(turned_imag, "seq", split_axis=0, concat_axis=1, tiled=True),
    )
    cos_local, sin_local = phase_table(tokens, tokens, tokens, -1.0, 0, 0)
    freq_real, freq_imag = transform(cos_local, sin_local, mid_real, mid_imag)
    moved_real, moved_imag = (
        lax.all_to_all(
            freq_real.reshape(2, parts, stride, channels),
            "seq",
            split_axis=1,
            concat_axis=0,
            tiled=True,
        ),
        lax.all_to_all(
            freq_imag.reshape(2, parts, stride, channels),
            "seq",
            split_axis=1,
            concat_axis=0,
            tiled=True,
        ),
    )
    moved_real = moved_real.reshape(2 * parts, stride, channels)
    moved_imag = moved_imag.reshape(2 * parts, stride, channels)
    local_filter = filter_spectra.reshape(stride, 2 * parts, 2, channels).astype(jnp.float32)
    spec_real = jnp.transpose(local_filter[:, :, 0, :], (1, 0, 2))
    spec_imag = jnp.transpose(local_filter[:, :, 1, :], (1, 0, 2))
    prod_real, prod_imag = complex_product(moved_real, moved_imag, spec_real, spec_imag)
    filt_real, filt_imag = (
        lax.all_to_all(prod_real, "seq", split_axis=0, concat_axis=1, tiled=True),
        lax.all_to_all(prod_imag, "seq", split_axis=0, concat_axis=1, tiled=True),
    )
    back_real, back_imag = transform(cos_local, -sin_local, filt_real, filt_imag)
    inv_cos, inv_sin = phase_table(2, tokens, points, 1.0, 2 * device_rank, 0)
    back_real, back_imag = complex_product(
        back_real, back_imag, inv_cos[:, :, None], inv_sin[:, :, None]
    )
    rows_real, rows_imag = (
        lax.all_to_all(
            back_real.reshape(2, parts, stride, channels),
            "seq",
            split_axis=1,
            concat_axis=0,
            tiled=True,
        ),
        lax.all_to_all(
            back_imag.reshape(2, parts, stride, channels),
            "seq",
            split_axis=1,
            concat_axis=0,
            tiled=True,
        ),
    )
    rows_real = rows_real.reshape(2 * parts, stride * channels)
    rows_imag = rows_imag.reshape(2 * parts, stride * channels)
    out_cos, out_sin = phase_table(parts, 2 * parts, 2 * parts, 1.0, 0, 0)
    positions = (
        jnp.dot(out_cos, rows_real, precision=exact_mode)
        - jnp.dot(out_sin, rows_imag, precision=exact_mode)
    ) * (1.0 / points)
    convolved = lax.all_to_all(
        positions.reshape(parts, stride, channels), "seq", split_axis=0, concat_axis=1, tiled=True
    ).reshape(tokens, channels)
    mixed_in = (
        gate_query.astype(jnp.float32) * (convolved + skip_gain[None, :] * gated_in)
    ).astype(jnp.bfloat16)
    partial_terms = jnp.dot(mixed_in, out_weight, preferred_element_type=jnp.float32)
    return lax.psum_scatter(partial_terms, "ch", scatter_dimension=1, tiled=True).astype(
        jnp.bfloat16
    )


def solution(mesh):
    placed = (
        P("seq", "ch"),
        P("seq", "ch"),
        P("seq", "ch"),
        P("ch"),
        P("seq", None, "ch"),
        P("ch", None),
    )
    return jax.shard_map(
        body, mesh=mesh, in_specs=placed, out_specs=P("seq", "ch"), check_vma=False
    )
```

profile of v0, /device:TPU:1, one launch (start us, length us, event | category | flops | bytes accessed | tf_op | source)
XLA Modules:
  0.0 495.2 jit_solution(7376907402544304677)
XLA Ops:
  6.5 2.3 convert_multiply_fusion
  8.9 8.6 %all-to-all-start = ((f32[32,16,512]{2,1,0:T(8,128)}), f32[32,16,512]{2,1,0:T(8,128)S(1)}, u32[]{:S(2)}, u32[]{:S(2)}) async-start(f32[32,16,512]{2,1,0:T(8,128)} %bitcast.1), calls=%async_computation | async-start | bytes 2097152 | tf_op jit(solution)/shard_map/all_to_all | solution.py:44
  17.5 0.1 fusion.74
  17.6 17.0 %all-to-all-done = f32[32,16,512]{2,1,0:T(8,128)S(1)} async-done(((f32[32,16,512]{2,1,0:T(8,128)}), f32[32,16,512]{2,1,0:T(8,128)S(1)}, u32[]{:S(2)}, u32[]{:S(2)}) %all-to-all-start) | async-done | bytes 1048608 | tf_op jit(solution)/shard_map/all_to_all | solution.py:44
  34.6 2.4 fusion.8
  37.1 2.8 multiply_subtract_fusion.1
  39.9 2.6 copy.35
  42.5 4.7 all-to-all-start.1
  47.2 2.6 copy.37
  49.8 25.4 %all-to-all-done.1 = f32[64,16,512]{2,1,0:T(8,128)} async-done(((f32[64,16,512]{2,1,0:T(8,128)}), f32[64,16,512]{2,1,0:T(8,128)}, u32[]{:S(2)}, u32[]{:S(2)}) %all-to-all-start.1) | async-done | bytes 2097184 | tf_op jit(solution)/shard_map/all_to_all | solution.py:60
  75.2 7.4 %all-to-all-start.2 = ((f32[64,16,512]{2,1,0:T(8,128)}), f32[64,16,512]{2,1,0:T(8,128)}, u32[]{:S(2)}, u32[]{:S(2)}) async-start(f32[64,16,512]{2,1,0:T(8,128)} %copy.37), calls=%async_computation.2 | async-start | bytes 4194304 | tf_op jit(solution)/shard_map/all_to_all | solution.py:61
  82.6 1.8 copy.36
  84.4 9.0 %fusion.22 = f32[2,512,512]{1,2,0:T(8,128)} fusion(f32[2,512,512]{2,1,0:T(8,128)S(1)} %bitcast.152), kind=kOutput, calls=%fused_computation.41 | convolution fusion | flops 3224895488 | bytes 4194304 | tf_op jit(solution)/shard_map/ks,gsc->gkc/dot_general | solution.py:20
  93.4 17.0 %all-to-all-done.2 = f32[64,16,512]{2,1,0:T(8,128)} async-done(((f32[64,16,512]{2,1,0:T(8,128)}), f32[64,16,512]{2,1,0:T(8,128)}, u32[]{:S(2)}, u32[]{:S(2)}) %all-to-all-start.2) | async-done | bytes 2097184 | tf_op jit(solution)/shard_map/all_to_all | solution.py:61
  110.4 2.0 copy.38
  112.4 0.2 copy-done.4
  112.6 7.4 %convolution_subtract_fusion.2 = f32[2,512,512]{1,2,0:T(8,128)S(1)} fusion(f32[2,512,512]{1,2,0:T(8,128)S(1)} %copy-done.4, f32[2,512,512]{2,1,0:T(8,128)S(1)} %bitcast.154), kind=kOutput, calls=%fused_computation.17 | convolution fusion | flops 3225419776 | bytes 6291456 | tf_op jit(solution)/shard_map/ks,gsc->gkc/dot_general | solution.py:20
  120.1 1.6 copy.39
  121.7 6.9 %all-to-all-start.3 = ((f32[2,32,16,512]{3,2,0,1:T(8,128)}), f32[2,32,16,512]{3,2,0,1:T(8,128)}, u32[]{:S(2)}, u32[]{:S(2)}) async-start(f32[2,32,16,512]{3,2,0,1:T(8,128)} %copy.39), calls=%async_computation.3 | async-start | bytes 4194304 | tf_op jit(solution)/shard_map/all_to_all | solution.py:66
  128.6 8.9 %fusion.20 = f32[2,512,512]{1,2,0:T(8,128)S(1)} fusion(f32[2,512,512]{2,1,0:T(8,128)} %bitcast.155), kind=kOutput, calls=%fused_computation.39 | convolution fusion | flops 3224895488 | bytes 4194304 | tf_op jit(solution)/shard_map/ks,gsc->gkc/dot_general | solution.py:20
  137.5 7.8 %convolution_add_fusion.1 = f32[2,512,512]{1,2,0:T(8,128)S(1)} fusion(f32[2,512,512]{1,2,0:T(8,128)S(1)} %fusion.20, f32[2,512,512]{2,1,0:T(8,128)S(1)} %bitcast.153), kind=kOutput, calls=%fused_computation.16 | convolution fusion | flops 3225419776 | bytes 6291456 | tf_op jit(solution)/shard_map/ks,gsc->gkc/dot_general | solution.py:20
  145.4 1.6 copy.42
  146.9 9.5 %all-to-all-done.3 = f32[2,32,16,512]{3,2,0,1:T(8,128)} async-done(((f32[2,32,16,512]{3,2,0,1:T(8,128)}), f32[2,32,16,512]{3,2,0,1:T(8,128)}, u32[]{:S(2)}, u32[]{:S(2)}) %all-to-all-start.3) | async-done | bytes 2097184 | tf_op jit(solution)/shard_map/all_to_all | solution.py:66
  156.4 6.1 %all-to-all-start.4 = ((f32[2,32,16,512]{3,2,0,1:T(8,128)}), f32[2,32,16,512]{3,2,0,1:T(8,128)S(1)}, u32[]{:S(2)}, u32[]{:S(2)}) async-start(f32[2,32,16,512]{3,2,0,1:T(8,128)} %copy.42), calls=%async_computation.4 | async-start | bytes 4194304 | tf_op jit(solution)/shard_map/all_to_all | solution.py:73
  162.5 1.9 copy.40
  164.4 2.6 fusion.125
  167.0 23.4 %all-to-all-done.4 = f32[2,32,16,512]{3,2,0,1:T(8,128)S(1)} async-done(((f32[2,32,16,512]{3,2,0,1:T(8,128)}), f32[2,32,16,512]{3,2,0,1:T(8,128)S(1)}, u32[]{:S(2)}, u32[]{:S(2)}) %all-to-all-start.4) | async-done | bytes 2097184 | tf_op jit(solution)/shard_map/all_to_all | solution.py:73
  190.4 6.8 %fusion.1 = (f32[64,16,512]{2,1,0:T(8,128)S(1)}, f32[64,16,512]{2,1,0:T(8,128)}) fusion(f32[2,32,16,512]{3,2,0,1:T(8,128)S(1)} %all-to-all-done.4, f32[2,32,16,512]{3,2,0,1:T(8,128)} %all-to-all-done.3, f32[16,64,1,512]{3,1,0,2:T(8,128)} %get-tuple-element.12, f32[16,64,1,512]{3,1,0,2:T(8,128)} %get-tuple-element.11), kind=kLoop, calls=%fused_computation.6 | loop fusion | flops 3145728 | bytes 12582912 | tf_op jit(solution)/shard_map/sub | solution.py:31
  197.2 34.2 %all_to_all.146 = f32[64,16,512]{2,1,0:T(8,128)} all-to-all(f32[64,16,512]{2,1,0:T(8,128)S(1)} %get-tuple-element.5), channel_id=1, replica_groups=mesh['seq'=32,'ch'=8] {'seq'}, dimensions={0} | all-to-all | bytes 4194304 | tf_op jit(solution)/shard_map/all_to_all | solution.py:88
  231.5 4.1 all-to-all-start.6
  235.5 0.2 fusion.76
  235.7 1.8 copy.44
  237.6 1.4 copy-done.1
  238.9 9.1 %fusion.18 = f32[2,512,512]{1,2,0:T(8,128)} fusion(f32[2,512,512]{2,1,0:T(8,128)S(1)} %bitcast.163), kind=kOutput, calls=%fused_computation.37 | convolution fusion | flops 3224895488 | bytes 4194304 | tf_op jit(solution)/shard_map/ks,gsc->gkc/dot_general | solution.py:20
  248.1 15.4 %all-to-all-done.6 = f32[64,16,512]{2,1,0:T(8,128)S(1)} async-done(((f32[64,16,512]{2,1,0:T(8,128)}), f32[64,16,512]{2,1,0:T(8,128)S(1)}, u32[]{:S(2)}, u32[]{:S(2)}) %all-to-all-start.6) | async-done | bytes 2097184 | tf_op jit(solution)/shard_map/all_to_all | solution.py:89
  263.5 0.2 copy.45
  263.7 0.0 copy-start.9
  263.7 7.3 %fusion.16 = f32[2,512,512]{1,2,0:T(8,128)S(1)} fusion(f32[2,512,512]{2,1,0:T(8,128)S(1)} %bitcast.169), kind=kOutput, calls=%fused_computation.35 | convolution fusion | flops 3224895488 | bytes 4194304 | tf_op jit(solution)/shard_map/ks,gsc->gkc/dot_general | solution.py:20
  271.0 0.0 copy-done.9
  271.0 7.7 %convolution_subtract_fusion.1 = f32[2,512,512]{1,2,0:T(8,128)S(1)} fusion(f32[2,512,512]{1,2,0:T(8,128)S(1)} %copy-done.9, f32[2,512,512]{2,1,0:T(8,128)S(1)} %bitcast.170), kind=kOutput, calls=%fused_computation.15 | convolution fusion | flops 3225681920 | bytes 6291456 | tf_op jit(solution)/shard_map/ks,gsc->gkc/dot_general | solution.py:20
  278.7 9.5 %multiply_add_fusion = (f32[2,512,512]{1,2,0:T(8,128)}, f32[2,512,512]{1,2,0:T(8,128)S(1)}) fusion(f32[2,512,512]{1,2,0:T(8,128)S(1)} %convolution_subtract_fusion.1, f32[2,512]{1,0:T(2,128)S(1)} %get-tuple-element.14, f32[2,512]{1,0:T(2,128)S(1)} %get-tuple-element.13, f32[2,512,512]{1,2,0:T(8,128)S(1)} %fusion.16, f32[2,512,512]{2,1,0:T(8,128)S(1)} %bitcast.164), kind=kOutput, calls=%fused_computation.10 | convolution fusion | flops 3228827648 | bytes 10493952 | tf_op jit(solution)/shard_map/ks,gsc->gkc/dot_general | solution.py:20
  288.2 1.6 copy.46
  289.8 6.0 %all-to-all-start.7 = ((f32[2,32,16,512]{3,2,0,1:T(8,128)}), f32[2,32,16,512]{3,2,0,1:T(8,128)S(1)}, u32[]{:S(2)}, u32[]{:S(2)}) async-start(f32[2,32,16,512]{3,2,0,1:T(8,128)} %copy.46), calls=%async_computation.7 | async-start | bytes 4194304 | tf_op jit(solution)/shard_map/all_to_all | solution.py:97
  295.9 3.3 copy.47
  299.1 24.7 %all-to-all-done.7 = f32[2,32,16,512]{3,2,0,1:T(8,128)S(1)} async-done(((f32[2,32,16,512]{3,2,0,1:T(8,128)}), f32[2,32,16,512]{3,2,0,1:T(8,128)S(1)}, u32[]{:S(2)}, u32[]{:S(2)}) %all-to-all-start.7) | async-done | bytes 2097184 | tf_op jit(solution)/shard_map/all_to_all | solution.py:97
  323.8 6.7 %all-to-all-start.8 = ((f32[2,32,16,512]{3,2,0,1:T(8,128)}), f32[2,32,16,512]{3,2,0,1:T(8,128)}, u32[]{:S(2)}, u32[]{:S(2)}) async-start(f32[2,32,16,512]{3,2,0,1:T(8,128)} %copy.47), calls=%async_computation.8 | async-start | bytes 4194304 | tf_op jit(solution)/shard_map/all_to_all | solution.py:104
  330.6 0.3 reduce-scatter.2.cloned.1.call-start
  330.9 1.2 copy.52
  332.1 1.2 fusion.54
  333.2 25.3 %all-to-all-done.8 = f32[2,32,16,512]{3,2,0,1:T(8,128)} async-done(((f32[2,32,16,512]{3,2,0,1:T(8,128)}), f32[2,32,16,512]{3,2,0,1:T(8,128)}, u32[]{:S(2)}, u32[]{:S(2)}) %all-to-all-start.8) | async-done | bytes 2097184 | tf_op jit(solution)/shard_map/all_to_all | solution.py:104
  358.5 2.8 copy.53
  361.3 1.2 fusion
  362.5 0.0 copy-start.5
  362.5 0.0 copy-start.6
  362.6 0.0 copy-start.7
  362.6 0.0 copy-start.8
  362.6 0.6 copy.54
  363.2 0.0 copy-start.3
  363.2 22.6 %all_to_all.147 = f32[32,16,512]{2,1,0:T(8,128)S(1)} all-to-all(f32[32,16,512]{2,1,0:T(8,128)S(1)} %bitcast.167), channel_id=1, replica_groups=mesh['seq'=32,'ch'=8] {'seq'}, dimensions={0} | all-to-all | bytes 2097152 | tf_op jit(solution)/shard_map/all_to_all | solution.py:119
  385.8 0.3 fusion.11
  386.2 5.6 %fusion.126 = f32[512,4096]{1,0:T(8,128)} fusion(bf16[512,512]{1,0:T(8,128)(2,1)S(1)} %fusion.11, bf16[512,4096]{1,0:T(8,128)(2,1)S(1)} %copy-done.3), kind=kOutput, calls=%fused_computation.149 | convolution fusion | flops 2147483648 | bytes 13107200 | tf_op jit(solution)/shard_map/dot_general | solution.py:125
  391.8 0.0 reduce-scatter.2.cloned.1.call-update
  391.8 94.0 %reduce-scatter.2.cloned.1.call-done = f32[512,512]{1,0:T(8,128)} async-done(((f32[512,4096]{1,0:T(8,128)}), f32[512,512]{1,0:T(8,128)}) %reduce-scatter.2.cloned.1.call-update) | async-done | bytes 1048592 | tf_op jit(solution)/shard_map/reduce_scatter | solution.py:126
  485.8 2.1 convert_element_type.79
  (13 shorter events, 0.0 us)
Async XLA Ops:
  8.9 25.8 %all-to-all-start = ((f32[32,16,512]{2,1,0:T(8,128)}), f32[32,16,512]{2,1,0:T(8,128)S(1)}, u32[]{:S(2)}, u32[]{:S(2)}) async-start(f32[32,16,512]{2,1,0:T(8,128)} %bitcast.1), calls=%async_computation | async-start | bytes 2097152 | tf_op jit(solution)/shard_map/all_to_all | solution.py:44
  42.5 32.7 %all-to-all-start.1 = ((f32[64,16,512]{2,1,0:T(8,128)}), f32[64,16,512]{2,1,0:T(8,128)}, u32[]{:S(2)}, u32[]{:S(2)}) async-start(f32[64,16,512]{2,1,0:T(8,128)} %copy.35), calls=%async_computation.1 | async-start | bytes 4194304 | tf_op jit(solution)/shard_map/all_to_all | solution.py:60
  75.2 35.2 %all-to-all-start.2 = ((f32[64,16,512]{2,1,0:T(8,128)}), f32[64,16,512]{2,1,0:T(8,128)}, u32[]{:S(2)}, u32[]{:S(2)}) async-start(f32[64,16,512]{2,1,0:T(8,128)} %copy.37), calls=%async_computation.2 | async-start | bytes 4194304 | tf_op jit(solution)/shard_map/all_to_all | solution.py:61
  110.4 2.2 copy-start.4
  112.4 7.6 %copy-start = (f32[32,2,16,512]{3,2,0,1:T(8,128)}, f32[32,2,16,512]{3,2,0,1:T(8,128)S(1)}, u32[]{:S(2)}) copy-start(f32[32,2,16,512]{3,2,0,1:T(8,128)S(1)} %copy.38) | copy-start | bytes 6291460
  121.7 34.7 %all-to-all-start.3 = ((f32[2,32,16,512]{3,2,0,1:T(8,128)}), f32[2,32,16,512]{3,2,0,1:T(8,128)}, u32[]{:S(2)}, u32[]{:S(2)}) async-start(f32[2,32,16,512]{3,2,0,1:T(8,128)} %copy.39), calls=%async_computation.3 | async-start | bytes 4194304 | tf_op jit(solution)/shard_map/all_to_all | solution.py:66
  156.4 34.0 %all-to-all-start.4 = ((f32[2,32,16,512]{3,2,0,1:T(8,128)}), f32[2,32,16,512]{3,2,0,1:T(8,128)S(1)}, u32[]{:S(2)}, u32[]{:S(2)}) async-start(f32[2,32,16,512]{3,2,0,1:T(8,128)} %copy.42), calls=%async_computation.4 | async-start | bytes 4194304 | tf_op jit(solution)/shard_map/all_to_all | solution.py:73
  231.5 32.0 %all-to-all-start.6 = ((f32[64,16,512]{2,1,0:T(8,128)}), f32[64,16,512]{2,1,0:T(8,128)S(1)}, u32[]{:S(2)}, u32[]{:S(2)}) async-start(f32[64,16,512]{2,1,0:T(8,128)} %get-tuple-element.6), calls=%async_computation.6 | async-start | bytes 4194304 | tf_op jit(solution)/shard_map/all_to_all | solution.py:89
  237.6 1.4 copy-start.1
  263.7 7.3 %copy-start.9 = (f32[2,512,512]{1,2,0:T(8,128)S(1)}, f32[2,512,512]{1,2,0:T(8,128)}, u32[]{:S(2)}) copy-start(f32[2,512,512]{1,2,0:T(8,128)} %fusion.18) | copy-start | bytes 6291460
  271.0 7.7 %copy-start.2 = (f32[2,32,16,512]{3,2,1,0:T(8,128)S(1)}, f32[2,32,16,512]{3,2,1,0:T(8,128)}, u32[]{:S(2)}) copy-start(f32[2,32,16,512]{3,2,1,0:T(8,128)} %copy-done.1) | copy-start | bytes 6291460
  289.8 34.0 %all-to-all-start.7 = ((f32[2,32,16,512]{3,2,0,1:T(8,128)}), f32[2,32,16,512]{3,2,0,1:T(8,128)S(1)}, u32[]{:S(2)}, u32[]{:S(2)}) async-start(f32[2,32,16,512]{3,2,0,1:T(8,128)} %copy.46), calls=%async_computation.7 | async-start | bytes 4194304 | tf_op jit(solution)/shard_map/all_to_all | solution.py:97
  323.8 34.7 %all-to-all-start.8 = ((f32[2,32,16,512]{3,2,0,1:T(8,128)}), f32[2,32,16,512]{3,2,0,1:T(8,128)}, u32[]{:S(2)}, u32[]{:S(2)}) async-start(f32[2,32,16,512]{3,2,0,1:T(8,128)} %copy.47), calls=%async_computation.8 | async-start | bytes 4194304 | tf_op jit(solution)/shard_map/all_to_all | solution.py:104
  330.6 155.3 %reduce-scatter.2.cloned.1.call-start = ((), (), s32[]{:S(2)}) async-start(), calls=%async_computation.11 | async-start | bytes 9437184 | tf_op jit(solution)/shard_map/reduce_scatter | solution.py:126
  362.5 23.3 %copy-start.5 = (bf16[512,512]{1,0:T(8,128)(2,1)S(1)}, bf16[512,512]{1,0:T(8,128)(2,1)}, u32[]{:S(2)}) copy-start(bf16[512,512]{1,0:T(8,128)(2,1)} %param.8) | copy-start | bytes 1572868
  362.5 23.3 %copy-start.6 = (bf16[512,512]{1,0:T(8,128)(2,1)S(1)}, bf16[512,512]{1,0:T(8,128)(2,1)}, u32[]{:S(2)}) copy-start(bf16[512,512]{1,0:T(8,128)(2,1)} %param.7) | copy-start | bytes 1572868
  362.6 23.3 %copy-start.7 = (bf16[512,512]{1,0:T(8,128)(2,1)S(1)}, bf16[512,512]{1,0:T(8,128)(2,1)}, u32[]{:S(2)}) copy-start(bf16[512,512]{1,0:T(8,128)(2,1)} %param.6) | copy-start | bytes 1572868
  362.6 23.3 %copy-start.8 = (f32[512]{0:T(512)S(1)}, f32[512]{0:T(512)}, u32[]{:S(2)}) copy-start(f32[512]{0:T(512)} %param.9) | copy-start | bytes 6148
  363.2 23.0 %copy-start.3 = (bf16[512,4096]{1,0:T(8,128)(2,1)S(1)}, bf16[512,4096]{1,0:T(8,128)(2,1)}, u32[]{:S(2)}) copy-start(bf16[512,4096]{1,0:T(8,128)(2,1)} %param.11) | copy-start | bytes 12582916
Sparse Core Ops, SparseCore 0:
  391.9 93.8 reduce-scatter.1
where the time goes:
time: 503 us; the launch traced here: 495 us
  waiting for transfers between devices  252 us (50%)
  matrix products  80 us (16%)
  blocking collectives  56.9 us (11%)
  starting transfers between devices  50.8 us (10%)
  local copies, waits for them, and re-layouts  29.8 us (6%)
  between operations  14.2 us (3%)
  other arithmetic  11.8 us (2%)
    reduce_scatter x1, waiting for transfers between devices, body(): lax.psum_scatter(partial_terms, 'ch', scatter_dimension=1, tiled=True)  94 us
    dot_general x8, matrix products, contract(): return jnp.einsum('ks,gsc->gkc', matrix, values, precision=exact_mode)  66.8 us
    all_to_all x1, blocking collectives, body(): lax.all_to_all(prod_real, 'seq', split_axis=0, concat_axis=1, tiled=True)  34.2 us
    all_to_all x1, waiting for transfers between devices, body(): lax.all_to_all(turned_real, 'seq', split_axis=0, concat_axis=1, tiled=True)  25.4 us
    all_to_all x1, waiting for transfers between devices, body(): lax.all_to_all(back_imag.reshape(2, parts, stride, channels), 'seq', spli...  25.3 us
    all_to_all x1, waiting for transfers between devices, body(): lax.all_to_all(back_real.reshape(2, parts, stride, channels), 'seq', spli...  24.7 us
    all_to_all x1, waiting for transfers between devices, body(): lax.all_to_all(freq_imag.reshape(2, parts, stride, channels), 'seq', spli...  23.4 us
    all_to_all x1, blocking collectives, body(): lax.all_to_all(positions.reshape(parts, stride, channels), 'seq', split_a...  22.6 us
  transfers between devices with their start and end apart: 9, of which 9 were waited for; matrix products, arithmetic and copies ran while one was open for 11% of the time, Pallas kernels for 0%

commit v1 on v0

v1 whole, which is shorter than its diff:
```python
import functools

import jax
import jax.numpy as jnp
import ml_dtypes
import numpy as np
from jax import lax
from jax.experimental import pallas as pl
from jax.experimental.pallas import tpu as pltpu
from jax.sharding import PartitionSpec as P

S = 32
C = 16
T = 512
R = 64
K = 512
LANES = 128
KL = 16
N = R * K
VMEM = pltpu.VMEM


def halves(table):
    table = np.asarray(table, np.float64)
    high = table.astype(ml_dtypes.bfloat16)
    low = (table - high.astype(np.float64)).astype(ml_dtypes.bfloat16)
    return high, low


@functools.lru_cache(None)
def tables():
    p, s = np.arange(R), np.arange(S)
    tau, kappa = np.arange(T), np.arange(K)
    cross = 2 * np.pi * np.outer(p, s) / R
    first = np.concatenate([np.cos(cross), -np.sin(cross)], 0)
    first = np.concatenate(halves(first), 1)
    turn = 2 * np.pi * np.outer(p, tau) / N
    inner = 2 * np.pi * (np.outer(kappa, tau) % K) / K
    inner = np.concatenate([np.cos(inner), np.sin(inner)], 1)
    inner_high, inner_low = halves(inner)
    last = np.concatenate([np.cos(cross).T, -np.sin(cross).T], 1) / N
    last_high, last_low = halves(last)
    last = np.concatenate([last_high, last_low, last_high], 1)
    order = np.zeros((2 * R, 2 * R), ml_dtypes.bfloat16)
    for q in range(R):
        for part in range(2):
            order[2 * q + part, part * R + q] = 1
    return dict(
        first=first,
        turn_cos=np.cos(turn).astype(np.float32),
        turn_sin=np.sin(turn).astype(np.float32),
        inner_high=inner_high,
        inner_low=inner_low,
        last=last,
        order=order,
    )


def dot(left, right, left_dim, right_dim):
    return lax.dot_general(
        left, right, (((left_dim,), (right_dim,)), ((), ())), preferred_element_type=jnp.float32
    )


def split(values):
    high = values.astype(jnp.bfloat16)
    return high, (values - high.astype(jnp.float32)).astype(jnp.bfloat16)


def prepare_kernel(key_ref, value_ref, spectra_ref, order_ref, gated_ref, filter_ref, wide):
    gated = key_ref[...].astype(jnp.float32) * value_ref[...].astype(jnp.float32)
    gated_ref[...] = gated.T.astype(jnp.bfloat16)

    @pl.loop(0, KL)
    def _(k):
        block = spectra_ref[pl.ds(pl.multiple_of(k * 2 * R, 2 * R), 2 * R), :]
        wide[pl.ds(k, T, stride=KL), :] = dot(block, order_ref[...], 0, 0)

    @pl.loop(0, T // C)
    def _(i):
        rows = pl.ds(pl.multiple_of(i * C * KL, C * KL), C * KL)
        filter_ref[rows, :] = wide[rows, :].astype(jnp.bfloat16)


def convolve_channel(gated, response, first, turn_cos, turn_sin, inner_high, inner_low, last):
    upper = dot(first, jnp.concatenate([gated, gated], 0), 1, 0)
    real, imag = upper[:R], upper[R:]
    turned_real = real * turn_cos + imag * turn_sin
    turned_imag = imag * turn_cos - real * turn_sin
    real_high, real_low = split(turned_real)
    imag_high, imag_low = split(turned_imag)
    high = jnp.concatenate(
        [jnp.concatenate([real_high, imag_high], 1), jnp.concatenate([imag_high, -real_high], 1)], 0
    )
    low = jnp.concatenate(
        [jnp.concatenate([real_low, imag_low], 1), jnp.concatenate([imag_low, -real_low], 1)], 0
    )
    spectrum = dot(inner_high, high, 1, 1) + (dot(inner_high, low, 1, 1) + dot(inner_low, high, 1, 1))
    lane = lax.broadcasted_iota(jnp.int32, (K, 2 * R), 1)
    is_real = lane < R
    swapped = pltpu.roll(response, R, 1)
    both_real = jnp.where(is_real, response, swapped)
    both_imag = jnp.where(is_real, -swapped, response)
    product = spectrum * both_real + pltpu.roll(spectrum, R, 1) * both_imag
    product_high, product_low = split(product)
    back = dot(product_high, inner_high, 0, 0) + (
        dot(product_low, inner_high, 0, 0) + dot(product_high, inner_low, 0, 0)
    )
    back_real = back[:R, :T] - back[R:, T:]
    back_imag = back[:R, T:] + back[R:, :T]
    out_real = back_real * turn_cos - back_imag * turn_sin
    out_imag = back_real * turn_sin + back_imag * turn_cos
    out_high, out_low = split(jnp.concatenate([out_real, out_imag], 0))
    return dot(last, jnp.concatenate([out_high, out_high, out_low], 0), 1, 0)


def convolve_kernel(
    gated_ref, filter_ref, first, turn_cos, turn_sin, inner_high, inner_low, last, out_ref, wide, result
):
    for i in range(T // LANES):
        lanes = slice(i * LANES, (i + 1) * LANES)
        wide[i] = gated_ref[:, :, lanes].reshape(S * C, LANES).astype(jnp.float32)

    @pl.loop(0, C)
    def _(c):
        rows = pl.ds(c, S, stride=C)
        gated = jnp.concatenate([wide[i, rows, :] for i in range(T // LANES)], 1)
        response = filter_ref[:, c].reshape(K, 2 * R).astype(jnp.float32)
        convolved = convolve_channel(
            gated.astype(jnp.bfloat16),
            response,
            first[...],
            turn_cos[...],
            turn_sin[...],
            inner_high[...],
            inner_low[...],
            last[...],
        )
        for i in range(T // LANES):
            result[i, rows, :] = convolved[:, i * LANES : (i + 1) * LANES]

    for i in range(T // LANES):
        lanes = slice(i * LANES, (i + 1) * LANES)
        out_ref[:, :, lanes] = result[i].astype(jnp.bfloat16).reshape(S, C, LANES)


def combine_kernel(conv_ref, query_ref, key_ref, value_ref, gain_ref, mixed_ref):
    gated = key_ref[...].astype(jnp.float32) * value_ref[...].astype(jnp.float32)
    convolved = conv_ref[...].astype(jnp.float32).T
    mixed = query_ref[...].astype(jnp.float32) * (convolved + gain_ref[...] * gated)
    mixed_ref[...] = mixed.astype(jnp.bfloat16)


def whole(count):
    return [pl.BlockSpec(memory_space=VMEM)] * count


def body(gate_query, gate_key, gate_value, skip_gain, filter_spectra, out_weight):
    tab = {name: jnp.asarray(table) for name, table in tables().items()}
    groups = lax.axis_size("ch")
    rank = lax.axis_index("seq")
    outputs = out_weight.shape[1] // groups
    params = pltpu.CompilerParams(vmem_limit_bytes=48 << 20)

    share = lax.dynamic_slice_in_dim(out_weight, rank * C, C, 0)
    share = lax.all_to_all(
        share.reshape(C, groups, outputs), "ch", split_axis=1, concat_axis=0, tiled=False
    )
    weight = lax.all_gather(share.reshape(groups, C, outputs), "seq", axis=0)
    weight = jnp.transpose(weight, (1, 0, 2, 3)).reshape(groups * T, outputs)

    gated, response = pl.pallas_call(
        prepare_kernel,
        out_shape=(
            jax.ShapeDtypeStruct((T, T), jnp.bfloat16),
            jax.ShapeDtypeStruct((T * KL, 2 * R), jnp.bfloat16),
        ),
        in_specs=whole(4),
        out_specs=tuple(whole(2)),
        scratch_shapes=[VMEM((T * KL, 2 * R), jnp.float32)],
        compiler_params=params,
    )(gate_key, gate_value, filter_spectra.reshape(KL * R * 2, T), tab["order"])
    gated = lax.all_to_all(gated.reshape(S, C, T), "seq", split_axis=0, concat_axis=0, tiled=True)
    response = lax.all_to_all(
        response.reshape(S, C, KL, 2 * R), "seq", split_axis=0, concat_axis=0, tiled=True
    )
    names = ("first", "turn_cos", "turn_sin", "inner_high", "inner_low", "last")
    convolved = pl.pallas_call(
        convolve_kernel,
        out_shape=jax.ShapeDtypeStruct((S, C, T), jnp.bfloat16),
        in_specs=whole(8),
        out_specs=whole(1)[0],
        scratch_shapes=[VMEM((T // LANES, S * C, LANES), jnp.float32)] * 2,
        compiler_params=params,
    )(gated, response, *(tab[name] for name in names))
    convolved = lax.all_to_all(convolved, "seq", split_axis=0, concat_axis=0, tiled=True)
    mixed = pl.pallas_call(
        combine_kernel,
        out_shape=jax.ShapeDtypeStruct((T, T), jnp.bfloat16),
        in_specs=whole(5),
        out_specs=whole(1)[0],
        compiler_params=params,
    )(convolved.reshape(S * C, T), gate_query, gate_key, gate_value, skip_gain[None, :])
    mixed = lax.all_gather(mixed, "ch", axis=1, tiled=True)
    return jnp.dot(mixed, weight, preferred_element_type=jnp.float32).astype(jnp.bfloat16)


def solution(mesh):
    placed = (
        P("seq", "ch"),
        P("seq", "ch"),
        P("seq", "ch"),
        P("ch"),
        P("seq", None, "ch"),
        P("ch", None),
    )
    return jax.shard_map(
        body, mesh=mesh, in_specs=placed, out_specs=P("seq", "ch"), check_vma=False
    )
```

time: 503 us -> 217 us (0.43); the launches traced: 495 us -> 217 us
  waiting for transfers between devices: 252 us -> 43.3 us
  matrix products: 80 us -> 6.59 us
  Pallas kernels: 0 us -> 51.5 us
  starting transfers between devices: 50.8 us -> 0.04 us
  blocking collectives: 56.9 us -> 93.3 us
  local copies, waits for them, and re-layouts: 29.8 us -> 8.69 us
  other arithmetic: 11.8 us -> 0 us
    all_to_all x8 -> x0, waiting for transfers between devices: 158 us -> none  [the longest x1 25.4 us: body(): lax.all_to_all(turned_real, 'seq', split_axis=0, concat_axis=1, tiled=True)]
    reduce_scatter x1 -> x0, waiting for transfers between devices: 94 us -> none  [body(): lax.psum_scatter(partial_terms, 'ch', scatter_dimension=1, tiled=True)]
    dot_general x13 -> x1, matrix products: 80 us -> 6.59 us  [body(): jnp.dot(mixed, weight, preferred_element_type=jnp.float32)]
    pallas_call x0 -> x3, Pallas kernels: none -> 51.5 us  [the longest x1 44.7 us: body(): pl.pallas_call(convolve_kernel, out_shape=jax.ShapeDtypeStruct((S, C, T),...]
    all_to_all x8 -> x0, starting transfers between devices: 50.5 us -> none  [the longest x1 8.59 us: body(): lax.all_to_all(gated_in.reshape(parts, stride, channels), 'seq', split_ax...]
    all_gather x0 -> x2, waiting for transfers between devices: none -> 43.3 us  [the longest x1 43.3 us: body(): mixed = lax.all_gather(mixed, 'ch', axis=1, tiled=True)]
    all_to_all x2 -> x4, blocking collectives: 56.9 us -> 93.3 us  [the longest x1 40.6 us: body(): lax.all_to_all(response.reshape(S, C, KL, 2 * R), 'seq', split_axis=0, co...]
    unnamed x24 -> x23, local copies, waits for them, and re-layouts: 8.13 us -> 0.11 us
  transfers between devices with their start and end apart: 9 -> 2, of which waited for: 9 -> 1; matrix products, arithmetic and copies ran while one was open for 11% -> 3% of each run, Pallas kernels for 0% -> 24%
where the time goes in v1:
time: 217 us
  blocking collectives  93.3 us (43%)
  Pallas kernels  51.5 us (24%)
  waiting for transfers between devices  43.3 us (20%)
  between operations  13.6 us (6%)
  local copies, waits for them, and re-layouts  8.69 us (4%)
  matrix products  6.59 us (3%)
    pallas_call x1, Pallas kernels, body(): pl.pallas_call(convolve_kernel, out_shape=jax.ShapeDtypeStruct((S, C, T),...  44.7 us
    all_gather x1, waiting for transfers between devices, body(): mixed = lax.all_gather(mixed, 'ch', axis=1, tiled=True)  43.3 us
    all_to_all x1, blocking collectives, body(): lax.all_to_all(response.reshape(S, C, KL, 2 * R), 'seq', split_axis=0, co...  40.6 us
    all_to_all x1, blocking collectives, body(): lax.all_to_all(gated.reshape(S, C, T), 'seq', split_axis=0, concat_axis=0...  21 us
    all_to_all x1, blocking collectives, body(): lax.all_to_all(share.reshape(C, groups, outputs), 'ch', split_axis=1, con...  16.7 us
    all_to_all x1, blocking collectives, body(): lax.all_to_all(convolved, 'seq', split_axis=0, concat_axis=0, tiled=True)  15.1 us
    dot_general x1, matrix products, body(): jnp.dot(mixed, weight, preferred_element_type=jnp.float32)  6.59 us
    pallas_call x1, Pallas kernels, body(): pl.pallas_call(prepare_kernel, out_shape=(jax.ShapeDtypeStruct((T, T), jn...  5.58 us
  transfers between devices with their start and end apart: 2, of which 1 were waited for; matrix products, arithmetic and copies ran while one was open for 3% of the time, Pallas kernels for 24%

profile of v1, /device:TPU:1, one launch (start us, length us, event | category | flops | bytes accessed | tf_op | source)
XLA Modules:
  0.0 217.1 jit_solution(8755472697664522168)
XLA Ops:
  6.5 0.0 copy-start.8
  6.5 0.0 copy-start.1
  6.5 0.0 copy-start
  6.5 0.0 all-gather.6.cloned.1.call-start
  6.5 1.0 constant_dynamic-slice_fusion
  7.6 16.7 %all_to_all.30 = bf16[1,16,8,512]{3,1,0,2:T(8,128)(2,1)} all-to-all(bf16[1,16,8,512]{3,1,0,2:T(8,128)(2,1)S(1)} %copy.19), channel_id=1, replica_groups=mesh['seq'=32,'ch'=8] {'ch'}, dimensions={2} | all-to-all | bytes 262144 | tf_op jit(solution)/shard_map/all_to_all | solution.py:166
  24.3 0.0 all-gather.6.cloned.1.call-update
  24.4 0.0 all-gather.4.cloned.1.call-start
  24.4 2.8 %reshape.16.spectra_ref = bf16[2048,512]{1,0:T(8,128)(2,1)S(1)} reshape(bf16[1024,2,512]{2,1,0:T(2,128)(2,1)} %param.17) | data formatting | bytes 4194304 | tf_op jit(solution)/shard_map/reshape | solution.py:182
  27.2 0.0 copy-done.8
  27.2 0.0 copy-done.1
  27.2 0.0 copy-done
  27.2 0.0 copy-start.2
  27.2 0.0 copy-start.3
  27.2 0.0 copy-start.5
  27.2 0.0 copy-start.6
  27.3 0.0 copy-start.7
  27.3 0.0 copy-start.9
  27.3 5.6 %shard_map.127 = (bf16[512,512]{1,0:T(8,128)(2,1)S(1)}, bf16[8192,128]{1,0:T(8,128)(2,1)S(1)}) custom-call(bf16[512,512]{1,0:T(8,128)(2,1)S(1)} %copy-done, bf16[512,512]{1,0:T(8,128)(2,1)S(1)} %copy-done.1, bf16[2048,512]{1,0:T(8,128)(2,1)S(1)} %reshape.16.spectra_ref, bf16[128,128]{1,0:T(8,128)(2,1)S(1)} %copy-done.8), custom_call_target="tpu_custom_call" | custom-call | tf_op jit(solution)/shard_map/pallas_call | solution.py:172
  32.9 21.0 %all_to_all.31.gated_ref = bf16[32,16,512]{2,1,0:T(8,128)(2,1)S(1)} all-to-all(bf16[32,16,512]{2,1,0:T(8,128)(2,1)S(1)} %bitcast.20), channel_id=1, replica_groups=mesh['seq'=32,'ch'=8] {'seq'}, dimensions={0} | all-to-all | bytes 1048576 | tf_op jit(solution)/shard_map/all_to_all | solution.py:183
  53.8 40.6 %all_to_all.32.filter_ref = bf16[32,16,16,128]{3,2,1,0:T(8,128)(2,1)S(1)} all-to-all(bf16[32,16,16,128]{3,2,1,0:T(8,128)(2,1)S(1)} %bitcast.18), channel_id=1, replica_groups=mesh['seq'=32,'ch'=8] {'seq'}, dimensions={0} | all-to-all | bytes 4194304 | tf_op jit(solution)/shard_map/all_to_all | solution.py:184
  94.4 0.0 copy-done.2
  94.4 0.0 copy-done.3
  94.4 0.0 copy-done.5
  94.4 0.0 copy-done.6
  94.4 0.0 copy-done.7
  94.5 0.0 copy-done.9
  94.5 0.0 copy-start.4
  94.5 0.0 copy-start.10
  94.5 44.7 %shard_map.128 = bf16[32,16,512]{2,1,0:T(8,128)(2,1)S(1)} custom-call(bf16[32,16,512]{2,1,0:T(8,128)(2,1)S(1)} %all_to_all.31.gated_ref, bf16[32,16,16,128]{3,2,1,0:T(8,128)(2,1)S(1)} %all_to_all.32.filter_ref, bf16[128,64]{1,0:T(8,128)(2,1)S(1)} %copy-done.7, f32[64,512]{1,0:T(8,128)S(1)} %copy-done.6, f32[64,512]{1,0:T(8,128)S(1)} %copy-done.5, ...), custom_call_target="tpu_custom_call" | custom-call | tf_op jit(solution)/shard_map/pallas_call | solution.py:188
  139.2 15.1 %all_to_all.33 = bf16[32,16,512]{2,1,0:T(8,128)(2,1)S(1)} all-to-all(bf16[32,16,512]{2,1,0:T(8,128)(2,1)S(1)} %shard_map.128), channel_id=1, replica_groups=mesh['seq'=32,'ch'=8] {'seq'}, dimensions={0} | all-to-all | bytes 1048576 | tf_op jit(solution)/shard_map/all_to_all | solution.py:196
  154.3 0.0 copy-done.4
  154.3 0.0 copy-done.10
  154.3 1.2 shard_map.129
  155.5 0.0 all-gather.4.cloned.1.call-update
  155.5 0.0 all-gather.6.cloned.1.call-done
  155.6 4.8 %copy.21 = bf16[8,32,16,512]{3,2,1,0:T(8,128)(2,1)} copy(bf16[8,32,16,512]{3,2,0,1:T(8,128)(2,1)} %bitcast.22) | data formatting | bytes 8388608 | tf_op jit(solution)/shard_map/transpose | solution.py:170
  160.4 43.3 %all-gather.4.cloned.1.call-done = bf16[512,4096]{1,0:T(8,128)(2,1)} async-done(((bf16[512,512]{1,0:T(8,128)(2,1)}), bf16[512,4096]{1,0:T(8,128)(2,1)}) %all-gather.4.cloned.1.call-update) | async-done | bytes 4194320 | tf_op jit(solution)/shard_map/all_gather | solution.py:204
  203.6 6.6 %convolution_convert_fusion = bf16[512,512]{1,0:T(8,128)(2,1)} fusion(bf16[512,4096]{1,0:T(8,128)(2,1)} %all-gather.4.cloned.1.call-done, bf16[4096,512]{1,0:T(8,128)(2,1)} %bitcast.23), kind=kOutput, calls=%fused_computation | convolution fusion | flops 2147745792 | bytes 8912896 | tf_op jit(solution)/shard_map/dot_general | solution.py:205
  (2 shorter events, 0.1 us)
Async XLA Ops:
  6.5 20.6 %copy-start.8 = (bf16[128,128]{1,0:T(8,128)(2,1)S(1)}, bf16[128,128]{1,0:T(8,128)(2,1)}, u32[]{:S(2)}) copy-start(bf16[128,128]{1,0:T(8,128)(2,1)} %constant.32.clone.order_ref) | copy-start | bytes 98308
  6.5 20.6 %copy-start.1 = (bf16[512,512]{1,0:T(8,128)(2,1)S(1)}, bf16[512,512]{1,0:T(8,128)(2,1)}, u32[]{:S(2)}) copy-start(bf16[512,512]{1,0:T(8,128)(2,1)} %value_ref.3) | copy-start | bytes 1572868
  6.5 20.7 %copy-start = (bf16[512,512]{1,0:T(8,128)(2,1)S(1)}, bf16[512,512]{1,0:T(8,128)(2,1)}, u32[]{:S(2)}) copy-start(bf16[512,512]{1,0:T(8,128)(2,1)} %key_ref.3) | copy-start | bytes 1572868
  6.5 149.0 %all-gather.6.cloned.1.call-start = ((), (), s32[]{:S(2)}) async-start(), calls=%async_computation.5 | async-start | bytes 4325376 | tf_op jit(solution)/shard_map/all_gather | solution.py:169
  24.4 179.3 %all-gather.4.cloned.1.call-start = ((), (), s32[]{:S(2)}) async-start(), calls=%async_computation.4 | async-start | bytes 4718592 | tf_op jit(solution)/shard_map/all_gather | solution.py:204
  27.2 67.2 %copy-start.2 = (bf16[512,1024]{1,0:T(8,128)(2,1)S(1)}, bf16[512,1024]{1,0:T(8,128)(2,1)}, u32[]{:S(2)}) copy-start(bf16[512,1024]{1,0:T(8,128)(2,1)} %constant.30.clone.inner_low) | copy-start | bytes 3145732
  27.2 67.2 %copy-start.3 = (bf16[512,1024]{1,0:T(8,128)(2,1)S(1)}, bf16[512,1024]{1,0:T(8,128)(2,1)}, u32[]{:S(2)}) copy-start(bf16[512,1024]{1,0:T(8,128)(2,1)} %constant.29.clone.inner_high) | copy-start | bytes 3145732
  27.2 67.2 %copy-start.5 = (f32[64,512]{1,0:T(8,128)S(1)}, f32[64,512]{1,0:T(8,128)}, u32[]{:S(2)}) copy-start(f32[64,512]{1,0:T(8,128)} %constant.28.clone.turn_sin) | copy-start | bytes 393220
  27.2 67.2 %copy-start.6 = (f32[64,512]{1,0:T(8,128)S(1)}, f32[64,512]{1,0:T(8,128)}, u32[]{:S(2)}) copy-start(f32[64,512]{1,0:T(8,128)} %constant.27.clone.turn_cos) | copy-start | bytes 393220
  27.3 67.2 %copy-start.7 = (bf16[128,64]{1,0:T(8,128)(2,1)S(1)}, bf16[128,64]{1,0:T(8,128)(2,1)}, u32[]{:S(2)}) copy-start(bf16[128,64]{1,0:T(8,128)(2,1)} %constant.26.clone.first) | copy-start | bytes 49156
  27.3 67.2 %copy-start.9 = (bf16[32,384]{1,0:T(8,128)(2,1)S(1)}, bf16[32,384]{1,0:T(8,128)(2,1)}, u32[]{:S(2)}) copy-start(bf16[32,384]{1,0:T(8,128)(2,1)} %constant.31.clone.last) | copy-start | bytes 73732
  94.5 59.9 %copy-start.4 = (bf16[512,512]{1,0:T(8,128)(2,1)S(1)}, bf16[512,512]{1,0:T(8,128)(2,1)}, u32[]{:S(2)}) copy-start(bf16[512,512]{1,0:T(8,128)(2,1)} %query_ref.1) | copy-start | bytes 1572868
  94.5 59.8 %copy-start.10 = (f32[512]{0:T(512)S(1)}, f32[512]{0:T(512)}, u32[]{:S(2)}) copy-start(f32[512]{0:T(512)} %param.16) | copy-start | bytes 6148
Sparse Core Ops, SparseCore 0:
  24.5 69.6 all-gather.5
  155.7 47.9 all-gather.3

commit v2 on v1

v2 whole, which is shorter than its diff:
```python
import functools

import jax
import jax.numpy as jnp
import ml_dtypes
import numpy as np
from jax import lax
from jax.experimental import pallas as pl
from jax.experimental.pallas import tpu as pltpu
from jax.sharding import PartitionSpec as P

S = 32
C = 16
Q = 4
G = C // Q
T = 512
R = 64
K = 512
L = 128
KL = K // S
N = R * K
MESH = pl.DeviceIdType.MESH
VMEM = pltpu.VMEM
BF16, F32 = jnp.bfloat16, jnp.float32


def halves(table):
    table = np.asarray(table, np.float64)
    high = table.astype(ml_dtypes.bfloat16)
    low = (table - high.astype(np.float64)).astype(ml_dtypes.bfloat16)
    return high, low


@functools.lru_cache(None)
def tables():
    p, s = np.arange(R), np.arange(S)
    tau, kappa = np.arange(T), np.arange(K)
    cross = 2 * np.pi * np.outer(p, s) / R
    each = np.eye(Q)
    first = np.concatenate([np.cos(cross), -np.sin(cross)], 0)
    first = np.concatenate(halves(np.kron(each, first)), 1)
    turn = 2 * np.pi * np.outer(p, tau) / N
    inner = 2 * np.pi * (np.outer(kappa, tau) % K) / K
    inner = np.concatenate([np.cos(inner), np.sin(inner)], 1)
    inner_high, inner_low = halves(inner)
    last = np.concatenate([np.cos(cross).T, -np.sin(cross).T], 1) / N
    last_high, last_low = halves(np.kron(each, last))
    last = np.concatenate([last_high, last_low, last_high], 1)
    order = np.zeros((2 * R, 2 * R), ml_dtypes.bfloat16)
    for q in range(R):
        for part in range(2):
            order[2 * q + part, part * R + q] = 1
    spread = np.zeros((T, T), ml_dtypes.bfloat16)
    gather = np.zeros((T, T), ml_dtypes.bfloat16)
    for j in range(S):
        for g in range(G):
            for c in range(Q):
                spread[j * C + g * Q + c, g * L + j * Q + c] = 1
                gather[(g * Q + c) * S + j, j * C + g * Q + c] = 1
    return dict(
        first=first,
        turn_cos=np.cos(turn).astype(np.float32),
        turn_sin=np.sin(turn).astype(np.float32),
        inner_high=inner_high,
        inner_low=inner_low,
        last=last,
        order=order,
        spread=spread,
        gather=gather,
    )


NAMES = (
    "first", "turn_cos", "turn_sin", "inner_high", "inner_low", "last", "order", "spread", "gather"
)


def dot(left, right, left_dim, right_dim):
    return lax.dot_general(
        left, right, (((left_dim,), (right_dim,)), ((), ())), preferred_element_type=F32
    )


def split(values):
    high = values.astype(BF16)
    return high, (values - high.astype(F32)).astype(BF16)


def chunk_lanes(g):
    return pl.ds(pl.multiple_of(g * L, L), L)


def seq_kernel(
    query, key, value, gain, spectra, first, turn_cos, turn_sin, inner_high, inner_low, last,
    order, spread, gather, mixed, gated_out, gated_in, filter_out, filter_in, conv_out, conv_in,
    wide, sorted_in, rows, spectrum, product, back, turned, staging, sent_gated, sent_filter,
    sent_conv, got_gated, got_filter, got_conv,
):
    me = lax.axis_index("seq")

    def peer(k):
        return lax.rem(me + k, S)

    barrier = pltpu.get_barrier_semaphore()

    @pl.loop(1, S)
    def _(k):
        pl.semaphore_signal(barrier, inc=1, device_id={"seq": peer(k)}, device_id_type=MESH)

    def send_all(source, target, sent, sem):
        @pl.loop(1, S)
        def _(k):
            pltpu.make_async_remote_copy(
                src_ref=source.at[peer(k)],
                dst_ref=target.at[me],
                send_sem=sent,
                recv_sem=sem,
                device_id={"seq": peer(k)},
                device_id_type=MESH,
            ).start()

        target[me] = source[me]

    def arrive(target, sem):
        most = target.at[pl.ds(0, S - 1)]
        pltpu.make_async_copy(most, most, sem).wait()

    def gated_values():
        return key[...].astype(F32) * value[...].astype(F32)

    def prepare_filter(g):
        @pl.loop(0, KL)
        def _(k):
            block = spectra[pl.ds(pl.multiple_of(k * 2 * R, 2 * R), 2 * R), chunk_lanes(g)]
            wide[pl.ds(k, L, stride=KL), :] = dot(block, order[...], 0, 0)

        filter_out[g] = wide[...].astype(BF16).reshape(S, Q, KL, L)

    gated_out[...] = (
        dot(spread[...], gated_values().astype(BF16), 1, 1).astype(BF16).reshape(S, C, T)
    )
    pl.semaphore_wait(barrier, S - 1)
    send_all(gated_out, gated_in, sent_gated, got_gated)

    @pl.loop(0, G)
    def _(g):
        prepare_filter(g)
        send_all(filter_out.at[g], filter_in.at[g], sent_filter.at[g], got_filter.at[g])

    arrive(gated_in, got_gated)
    sorted_in[...] = dot(gather[...], gated_in[...].reshape(T, T), 1, 0).astype(BF16)

    @pl.loop(0, G)
    def _(g):
        values = sorted_in[pl.ds(pl.multiple_of(g * L, L), L), :]
        back[:, :T] = dot(first[...], jnp.concatenate([values, values], 0), 1, 0)
        for c in range(Q):
            at = c * 2 * R
            real, imag = back[at : at + R, :T], back[at + R : at + 2 * R, :T]
            turned_real = (real * turn_cos[...] + imag * turn_sin[...]).astype(BF16)
            turned_imag = (imag * turn_cos[...] - real * turn_sin[...]).astype(BF16)
            rows[at : at + R, :T] = turned_real
            rows[at : at + R, T:] = turned_imag
            rows[at + R : at + 2 * R, :T] = turned_imag
            rows[at + R : at + 2 * R, T:] = -turned_real
        spectrum[g] = dot(inner_high[...], rows[...], 1, 1) + dot(inner_low[...], rows[...], 1, 1)

    def convolve(g):
        arrive(filter_in.at[g], got_filter.at[g])
        is_real = lax.broadcasted_iota(jnp.int32, (K, L), 1) < R
        for c in range(Q):
            lanes = slice(c * L, (c + 1) * L)
            response = filter_in[g, :, c].reshape(K, L).astype(F32)
            swapped = pltpu.roll(response, R, 1)
            value_c = spectrum[g, :, lanes]
            product[:, lanes] = (
                value_c * jnp.where(is_real, response, swapped)
                + pltpu.roll(value_c, R, 1) * jnp.where(is_real, -swapped, response)
            ).astype(BF16)
        back[...] = dot(product[...], inner_high[...], 0, 0) + dot(product[...], inner_low[...], 0, 0)
        for c in range(Q):
            at = c * 2 * R
            real = back[at : at + R, :T] - back[at + R : at + 2 * R, T:]
            imag = back[at : at + R, T:] + back[at + R : at + 2 * R, :T]
            for at, part in (
                (at, real * turn_cos[...] - imag * turn_sin[...]),
                (at + R, real * turn_sin[...] + imag * turn_cos[...]),
            ):
                high, low = split(part)
                turned[at : at + R, :] = high
                turned[T + at : T + at + R, :] = high
                turned[2 * T + at : 2 * T + at + R, :] = low
        result = dot(last[...], turned[...], 1, 0)
        for c in range(Q):
            for i in range(T // L):
                staging[pl.ds(c * Q + i, S, stride=C), :] = result[
                    c * S : (c + 1) * S, i * L : (i + 1) * L
                ]
        conv_out[g] = staging[...].astype(BF16).reshape(S, C, L)
        send_all(conv_out.at[g], conv_in.at[g], sent_conv.at[g], got_conv.at[g])

    def combine(g):
        arrive(conv_in.at[g], got_conv.at[g])
        staging[...] = conv_in[g].reshape(T, L).astype(F32)
        lanes = chunk_lanes(g)
        for i in range(T // L):
            tokens = slice(i * L, (i + 1) * L)
            convolved = staging[pl.ds(i, L, stride=Q), :].T
            gated = key[tokens, lanes].astype(F32) * value[tokens, lanes].astype(F32)
            mixed[tokens, lanes] = (
                query[tokens, lanes].astype(F32) * (convolved + gain[:, lanes] * gated)
            ).astype(BF16)

    convolve(0)

    @pl.loop(1, G)
    def _(g):
        convolve(g)
        combine(g - 1)

    combine(G - 1)
    arrive(gated_out, sent_gated)
    for g in range(G):
        arrive(filter_out.at[g], sent_filter.at[g])
        arrive(conv_out.at[g], sent_conv.at[g])


def whole(count):
    return [pl.BlockSpec(memory_space=VMEM)] * count


def body(gate_query, gate_key, gate_value, skip_gain, filter_spectra, out_weight):
    tab = tables()
    groups = lax.axis_size("ch")
    rank = lax.axis_index("seq")
    outputs = out_weight.shape[1] // groups

    share = lax.dynamic_slice_in_dim(out_weight, rank * C, C, 0)
    share = lax.all_to_all(
        share.reshape(C, groups, outputs), "ch", split_axis=1, concat_axis=0, tiled=False
    )
    weight = lax.all_gather(share.reshape(groups, C, outputs), "seq", axis=0)
    weight = jnp.transpose(weight, (1, 0, 2, 3)).reshape(groups * T, outputs)

    dma = pltpu.SemaphoreType.DMA
    mixed = pl.pallas_call(
        seq_kernel,
        out_shape=jax.ShapeDtypeStruct((T, T), BF16),
        in_specs=whole(5 + len(NAMES)),
        out_specs=whole(1)[0],
        scratch_shapes=[
            VMEM((S, C, T), BF16),
            VMEM((S, C, T), BF16),
            VMEM((G, S, Q, KL, L), BF16),
            VMEM((G, S, Q, KL, L), BF16),
            VMEM((G, S, C, L), BF16),
            VMEM((G, S, C, L), BF16),
            VMEM((L * KL, L), F32),
            VMEM((T, T), BF16),
            VMEM((T, 2 * T), BF16),
            VMEM((G, K, T), F32),
            VMEM((K, T), BF16),
            VMEM((T, 2 * T), F32),
            VMEM((3 * T, T), BF16),
            VMEM((T, L), F32),
            dma(()),
            dma((G,)),
            dma((G,)),
            dma(()),
            dma((G,)),
            dma((G,)),
        ],
        compiler_params=pltpu.CompilerParams(
            collective_id=0, has_side_effects=True, vmem_limit_bytes=52 << 20
        ),
        cost_estimate=pl.CostEstimate(flops=12 * 10**9, bytes_accessed=8 << 20, transcendentals=0),
    )(
        gate_query,
        gate_key,
        gate_value,
        skip_gain[None, :],
        filter_spectra.reshape(KL * R * 2, T),
        *(jnp.asarray(tab[name]) for name in NAMES),
    )
    mixed = lax.all_gather(mixed, "ch", axis=1, tiled=True)
    return jnp.dot(mixed, weight, preferred_element_type=F32).astype(BF16)


def solution(mesh):
    placed = (
        P("seq", "ch"),
        P("seq", "ch"),
        P("seq", "ch"),
        P("ch"),
        P("seq", None, "ch"),
        P("ch", None),
    )
    return jax.shard_map(
        body, mesh=mesh, in_specs=placed, out_specs=P("seq", "ch"), check_vma=False
    )
```

time: 217 us -> 160 us (0.74)
  blocking collectives: 93.3 us -> 16.7 us
  waiting for transfers between devices: 43.3 us -> 55.3 us
  Pallas kernels: 51.5 us -> 57.8 us
    all_to_all x3 -> x0, blocking collectives: 76.6 us -> none  [the longest x1 40.6 us: body(): lax.all_to_all(response.reshape(S, C, KL, 2 * R), 'seq', split_axis=0, co...]
    all_gather x1, waiting for transfers between devices: 43.3 us -> 50.2 us  [body(): mixed = lax.all_gather(mixed, 'ch', axis=1, tiled=True)]
    pallas_call x3 -> x1, Pallas kernels: 51.5 us -> 57.8 us  [body(): pl.pallas_call(seq_kernel, out_shape=jax.ShapeDtypeStruct((T, T), BF16),...]
    all_gather x1, waiting for transfers between devices: 0.02 us -> 5.1 us  [body(): weight = lax.all_gather(share.reshape(groups, C, outputs), 'seq', axis=0)]
  transfers between devices with their start and end apart: 2 -> 2, of which waited for: 1 -> 2; matrix products, arithmetic and copies ran while one was open for 3% -> 6% of each run, Pallas kernels for 24% -> 36%
where the time goes in v2:
time: 160 us
  Pallas kernels  57.8 us (36%)
  waiting for transfers between devices  55.3 us (35%)
  blocking collectives  16.7 us (10%)
  between operations  13.5 us (8%)
  local copies, waits for them, and re-layouts  10 us (6%)
  matrix products  6.59 us (4%)
    pallas_call x1, Pallas kernels, body(): pl.pallas_call(seq_kernel, out_shape=jax.ShapeDtypeStruct((T, T), BF16),...  57.8 us
    all_gather x1, waiting for transfers between devices, body(): mixed = lax.all_gather(mixed, 'ch', axis=1, tiled=True)  50.2 us
    all_to_all x1, blocking collectives, body(): lax.all_to_all(share.reshape(C, groups, outputs), 'ch', split_axis=1, con...  16.7 us
    dot_general x1, matrix products, body(): return jnp.dot(mixed, weight, preferred_element_type=F32).astype(BF16)  6.59 us
    all_gather x1, waiting for transfers between devices, body(): weight = lax.all_gather(share.reshape(groups, C, outputs), 'seq', axis=0)  5.1 us
    transpose x1, local copies, waits for them, and re-layouts, body(): weight = jnp.transpose(weight, (1, 0, 2, 3)).reshape(groups * T, outputs)  4.77 us
    reshape x1, local copies, waits for them, and re-layouts, body(): filter_spectra.reshape(KL * R * 2, T)  4.11 us
  transfers between devices with their start and end apart: 2, of which 2 were waited for; matrix products, arithmetic and copies ran while one was open for 6% of the time, Pallas kernels for 36%

profile of v2, /device:TPU:1, one launch (start us, length us, event | category | flops | bytes accessed | tf_op | source)
XLA Modules:
  0.0 160.0 jit_solution(1616421683646193281)
XLA Ops:
  6.5 0.0 copy-start.6
  6.5 0.0 copy-start.2
  6.5 0.0 copy-start.4
  6.5 0.0 copy-start.5
  6.5 0.0 copy-start.3
  6.6 0.0 copy-start.1
  6.6 0.0 copy-start
  6.6 0.0 all-gather.6.cloned.1.call-start
  6.6 1.0 constant_dynamic-slice_fusion
  7.7 16.7 %all_to_all.15 = bf16[1,16,8,512]{3,1,0,2:T(8,128)(2,1)} all-to-all(bf16[1,16,8,512]{3,1,0,2:T(8,128)(2,1)S(1)} %copy.21), channel_id=1, replica_groups=mesh['seq'=32,'ch'=8] {'ch'}, dimensions={2} | all-to-all | bytes 262144 | tf_op jit(solution)/shard_map/all_to_all | solution.py:239
  24.4 0.0 all-gather.6.cloned.1.call-update
  24.5 0.0 all-gather.4.cloned.1.call-start
  24.5 4.1 %reshape.7.spectra = bf16[2048,512]{1,0:T(8,128)(2,1)} reshape(bf16[1024,2,512]{2,1,0:T(2,128)(2,1)} %param.19) | data formatting | bytes 4194304 | tf_op jit(solution)/shard_map/reshape | solution.py:282
  28.6 0.0 copy-done.6
  28.6 0.0 copy-done.2
  28.6 0.0 copy-done.4
  28.6 0.0 copy-done.5
  28.6 0.0 copy-done.3
  28.6 0.0 copy-done.1
  28.7 0.0 copy-done
  28.7 57.8 %shard_map.145 = bf16[512,512]{1,0:T(8,128)(2,1)} custom-call(bf16[512,512]{1,0:T(8,128)(2,1)S(1)} %copy-done, bf16[512,512]{1,0:T(8,128)(2,1)} %key.1, bf16[512,512]{1,0:T(8,128)(2,1)} %value.1, f32[1,512]{1,0:T(1,128)S(1)} %bitcast.15, bf16[2048,512]{1,0:T(8,128)(2,1)} %reshape.7.spectra, bf16[512,256]{1,0:T(8,128)(2,1)S(1)} %copy-done.3, ...), custom_call_target="tpu_custom_call" | custom-call | flops 12000000000 | bytes 8388608 | tf_op jit(solution)/shard_map/pallas_call | solution.py:246
  86.5 0.0 all-gather.4.cloned.1.call-update
  86.5 5.1 %all-gather.6.cloned.1.call-done = bf16[256,1,16,1,512]{4,2,3,1,0:T(8,128)(2,1)} async-done(((bf16[8,1,16,1,512]{4,2,3,1,0:T(8,128)(2,1)}), bf16[256,1,16,1,512]{4,2,3,1,0:T(8,128)(2,1)}) %all-gather.6.cloned.1.call-update) | async-done | bytes 4194320 | tf_op jit(solution)/shard_map/all_gather | solution.py:242
  91.6 4.8 %copy.23 = bf16[8,32,16,512]{3,2,1,0:T(8,128)(2,1)} copy(bf16[8,32,16,512]{3,2,0,1:T(8,128)(2,1)} %bitcast.16) | data formatting | bytes 8388608 | tf_op jit(solution)/shard_map/transpose | solution.py:243
  96.4 50.2 %all-gather.4.cloned.1.call-done = bf16[512,4096]{1,0:T(8,128)(2,1)} async-done(((bf16[512,512]{1,0:T(8,128)(2,1)}), bf16[512,4096]{1,0:T(8,128)(2,1)}) %all-gather.4.cloned.1.call-update) | async-done | bytes 4194320 | tf_op jit(solution)/shard_map/all_gather | solution.py:285
  146.6 6.6 %convolution_convert_fusion = bf16[512,512]{1,0:T(8,128)(2,1)} fusion(bf16[512,4096]{1,0:T(8,128)(2,1)} %all-gather.4.cloned.1.call-done, bf16[4096,512]{1,0:T(8,128)(2,1)} %bitcast.17), kind=kOutput, calls=%fused_computation | convolution fusion | flops 2147745792 | bytes 8912896 | tf_op jit(solution)/shard_map/dot_general | solution.py:286
  (2 shorter events, 0.1 us)
Async XLA Ops:
  6.5 22.1 %copy-start.6 = (bf16[128,128]{1,0:T(8,128)(2,1)S(1)}, bf16[128,128]{1,0:T(8,128)(2,1)}, u32[]{:S(2)}) copy-start(bf16[128,128]{1,0:T(8,128)(2,1)} %constant.36.clone.order) | copy-start | bytes 98308
  6.5 22.1 %copy-start.2 = (bf16[128,1536]{1,0:T(8,128)(2,1)S(1)}, bf16[128,1536]{1,0:T(8,128)(2,1)}, u32[]{:S(2)}) copy-start(bf16[128,1536]{1,0:T(8,128)(2,1)} %constant.35.clone.last) | copy-start | bytes 1179652
  6.5 22.1 %copy-start.4 = (f32[64,512]{1,0:T(8,128)S(1)}, f32[64,512]{1,0:T(8,128)}, u32[]{:S(2)}) copy-start(f32[64,512]{1,0:T(8,128)} %constant.32.clone.turn_sin) | copy-start | bytes 393220
  6.5 22.1 %copy-start.5 = (f32[64,512]{1,0:T(8,128)S(1)}, f32[64,512]{1,0:T(8,128)}, u32[]{:S(2)}) copy-start(f32[64,512]{1,0:T(8,128)} %constant.31.clone.turn_cos) | copy-start | bytes 393220
  6.5 22.1 %copy-start.3 = (bf16[512,256]{1,0:T(8,128)(2,1)S(1)}, bf16[512,256]{1,0:T(8,128)(2,1)}, u32[]{:S(2)}) copy-start(bf16[512,256]{1,0:T(8,128)(2,1)} %constant.30.clone.first) | copy-start | bytes 786436
  6.6 22.1 %copy-start.1 = (f32[512]{0:T(512)S(1)}, f32[512]{0:T(512)}, u32[]{:S(2)}) copy-start(f32[512]{0:T(512)} %param.18) | copy-start | bytes 6148
  6.6 22.1 %copy-start = (bf16[512,512]{1,0:T(8,128)(2,1)S(1)}, bf16[512,512]{1,0:T(8,128)(2,1)}, u32[]{:S(2)}) copy-start(bf16[512,512]{1,0:T(8,128)(2,1)} %query.1) | copy-start | bytes 1572868
  6.6 85.1 %all-gather.6.cloned.1.call-start = ((), (), s32[]{:S(2)}) async-start(), calls=%async_computation.2 | async-start | bytes 4325376 | tf_op jit(solution)/shard_map/all_gather | solution.py:242
  24.5 122.1 %all-gather.4.cloned.1.call-start = ((), (), s32[]{:S(2)}) async-start(), calls=%async_computation.1 | async-start | bytes 4718592 | tf_op jit(solution)/shard_map/all_gather | solution.py:285
Sparse Core Ops, SparseCore 0:
  24.6 67.0 all-gather.5
  93.4 53.0 all-gather.3

commit v3 on v2

--- a/solution.py
+++ b/solution.py
@@ -10,6 +10,7 @@
 from jax.sharding import PartitionSpec as P
 
 S = 32
+Z = 8
 C = 16
 Q = 4
 G = C // Q
@@ -46,10 +47,11 @@
     last = np.concatenate([np.cos(cross).T, -np.sin(cross).T], 1) / N
     last_high, last_low = halves(np.kron(each, last))
     last = np.concatenate([last_high, last_low, last_high], 1)
-    order = np.zeros((2 * R, 2 * R), ml_dtypes.bfloat16)
+    order = np.zeros((2 * R * G, 2 * R * G), ml_dtypes.bfloat16)
     for q in range(R):
-        for part in range(2):
-            order[2 * q + part, part * R + q] = 1
+        for g in range(G):
+            for part in range(2):
+                order[(q * G + g) * 2 + part, (g * 2 + part) * R + q] = 1
     spread = np.zeros((T, T), ml_dtypes.bfloat16)
     gather = np.zeros((T, T), ml_dtypes.bfloat16)
     for j in range(S):
@@ -90,63 +92,165 @@
     return pl.ds(pl.multiple_of(g * L, L), L)
 
 
-def seq_kernel(
-    query, key, value, gain, spectra, first, turn_cos, turn_sin, inner_high, inner_low, last,
-    order, spread, gather, mixed, gated_out, gated_in, filter_out, filter_in, conv_out, conv_in,
-    wide, sorted_in, rows, spectrum, product, back, turned, staging, sent_gated, sent_filter,
-    sent_conv, got_gated, got_filter, got_conv,
+def kernel(
+    query, key, value, gain, spectra, weight_here, first, turn_cos, turn_sin, inner_high, inner_low,
+    last, order, spread, gather, out, gated_out, gated_in, filter_out, filter_in, conv_out, conv_in,
+    share, weight, mixed, wide, sorted_in, rows, spectrum, product, back, turned, staging, local,
+    sent_gated, sent_filter, sent_conv, sent_share, sent_weight, sent_ring, got_gated, got_filter,
+    got_conv, got_share, got_weight, got_ring,
 ):
-    me = lax.axis_index("seq")
+    me, level = lax.axis_index("seq"), lax.axis_index("ch")
+    core, x, y = lax.rem(me, 2), lax.rem(me // 2, 4), me // 8
+    sibling = me + 1 - 2 * core
 
     def peer(k):
         return lax.rem(me + k, S)
 
+    def at_level(k):
+        return lax.rem(level + k + Z, Z)
+
+    def along_x(k):
+        return y * 8 + lax.rem(x + k, 4) * 2 + core
+
+    def along_y(k):
+        return lax.rem(y + k, 4) * 8 + x * 2 + core
+
+    share_load = pltpu.make_async_copy(
+        weight_here.at[pl.ds(pl.multiple_of(me * C, C), C), :], share, local
+    )
+    share_load.start()
     barrier = pltpu.get_barrier_semaphore()
 
     @pl.loop(1, S)
     def _(k):
         pl.semaphore_signal(barrier, inc=1, device_id={"seq": peer(k)}, device_id_type=MESH)
 
-    def send_all(source, target, sent, sem):
+    @pl.loop(1, Z)
+    def _(k):
+        pl.semaphore_signal(barrier, inc=1, device_id={"ch": at_level(k)}, device_id_type=MESH)
+
+    def send(source, target, sent, got, **to):
+        pltpu.make_async_remote_copy(
+            src_ref=source, dst_ref=target, send_sem=sent, recv_sem=got, device_id=to,
+            device_id_type=MESH,
+        ).start()
+
+    def send_all(source, target, sent, got):
         @pl.loop(1, S)
         def _(k):
-            pltpu.make_async_remote_copy(
-                src_ref=source.at[peer(k)],
-                dst_ref=target.at[me],
-                send_sem=sent,
-                recv_sem=sem,
-                device_id={"seq": peer(k)},
-                device_id_type=MESH,
-            ).start()
+            send(source.at[peer(k)], target.at[me], sent, got, seq=peer(k))
 
         target[me] = source[me]
 
+    def wait(ref, sem):
+        pltpu.make_async_copy(ref, ref, sem).wait()
+
     def arrive(target, sem):
-        most = target.at[pl.ds(0, S - 1)]
-        pltpu.make_async_copy(most, most, sem).wait()
+        wait(target.at[pl.ds(0, S - 1)], sem)
+
+    def share_lanes(k):
+        return pl.ds(pl.multiple_of(k * T, T), T)
+
+    def spread_share():
+        @pl.loop(1, Z)
+        def _(k):
+            to = at_level(k)
+            send(
+                share.at[:, share_lanes(to)], weight.at[level, me], sent_share, got_share, ch=to
+            )
+
+        weight[level, me] = share[:, share_lanes(level)]
+
+    lower, upper = pl.ds(0, Z // 2), pl.ds(Z // 2, Z // 2)
+
+    def weight_first():
+        wait(weight.at[pl.ds(0, Z - 1), 0], got_share)
+
+        @pl.loop(1, 4)
+        def _(k):
+            part = weight.at[lower, me]
+            send(part, part, sent_weight.at[0], got_weight.at[0], seq=along_x(k))
+            part = weight.at[upper, me]
+            send(part, part, sent_weight.at[1], got_weight.at[1], seq=along_y(k))
+
+    def weight_second():
+        wait(weight.at[lower, pl.ds(0, 3)], got_weight.at[0])
+        wait(weight.at[upper, pl.ds(0, 3)], got_weight.at[1])
+
+        @pl.loop(1, 4)
+        def _(k):
+            @pl.loop(0, 4)
+            def _(i):
+                part = weight.at[lower, along_x(i)]
+                send(part, part, sent_weight.at[2], got_weight.at[2], seq=along_y(k))
+                part = weight.at[upper, along_y(i)]
+                send(part, part, sent_weight.at[3], got_weight.at[3], seq=along_x(k))
+
+    def weight_third():
+        wait(weight.at[lower, pl.ds(0, 12)], got_weight.at[2])
+        wait(weight.at[upper, pl.ds(0, 12)], got_weight.at[3])
+
+        @pl.loop(0, S // 2)
+        def _(i):
+            part = weight.at[:, 2 * i + core]
+            send(part, part, sent_weight.at[4], got_weight.at[4], seq=sibling)
+
+    def weight_sent():
+        wait(weight.at[pl.ds(0, Z - 1), 0], sent_share)
+        wait(weight.at[lower, pl.ds(0, 3)], sent_weight.at[0])
+        wait(weight.at[upper, pl.ds(0, 3)], sent_weight.at[1])
+        wait(weight.at[lower, pl.ds(0, 12)], sent_weight.at[2])
+        wait(weight.at[upper, pl.ds(0, 12)], sent_weight.at[3])
+        wait(weight.at[:, pl.ds(0, S // 2)], sent_weight.at[4])
+
+    def ring_part(way, hop, g, source):
+        tokens = pl.ds(0, T)
+        if hop == Z // 2:
+            tokens = pl.ds(way * (T // 2), T // 2)
+        return mixed.at[source, tokens, chunk_lanes(g)]
+
+    def ring_send(hop, g):
+        for way, sign in enumerate((1, -1)):
+            part = ring_part(way, hop, g, at_level(-sign * (hop - 1)))
+            send(
+                part, part, sent_ring.at[way, hop - 1, g], got_ring.at[way, hop - 1, g],
+                ch=at_level(sign),
+            )
+
+    def ring_arrive(hop, g):
+        for way, sign in enumerate((1, -1)):
+            wait(ring_part(way, hop, g, at_level(-sign * hop)), got_ring.at[way, hop - 1, g])
+
+    def forward(hop, g):
+        ring_arrive(hop - 1, g)
+        ring_send(hop, g)
 
     def gated_values():
         return key[...].astype(F32) * value[...].astype(F32)
 
-    def prepare_filter(g):
+    def prepare_filter():
         @pl.loop(0, KL)
         def _(k):
-            block = spectra[pl.ds(pl.multiple_of(k * 2 * R, 2 * R), 2 * R), chunk_lanes(g)]
-            wide[pl.ds(k, L, stride=KL), :] = dot(block, order[...], 0, 0)
-
-        filter_out[g] = wide[...].astype(BF16).reshape(S, Q, KL, L)
+            block = spectra[pl.ds(pl.multiple_of(k * T, T), T), :]
+            moved = dot(block, order[...], 0, 0)
+            for g in range(G):
+                wide[g, pl.ds(k, L, stride=KL), :] = moved[:, g * L : (g + 1) * L]
 
     gated_out[...] = (
         dot(spread[...], gated_values().astype(BF16), 1, 1).astype(BF16).reshape(S, C, T)
     )
-    pl.semaphore_wait(barrier, S - 1)
+    pl.semaphore_wait(barrier, S + Z - 2)
     send_all(gated_out, gated_in, sent_gated, got_gated)
+    share_load.wait()
+    spread_share()
+    prepare_filter()
 
     @pl.loop(0, G)
     def _(g):
-        prepare_filter(g)
+        filter_out[g] = wide[g].astype(BF16).reshape(S, Q, KL, L)
         send_all(filter_out.at[g], filter_in.at[g], sent_filter.at[g], got_filter.at[g])
 
+    weight_first()
     arrive(gated_in, got_gated)
     sorted_in[...] = dot(gather[...], gated_in[...].reshape(T, T), 1, 0).astype(BF16)
 
@@ -207,22 +311,61 @@
             tokens = slice(i * L, (i + 1) * L)
             convolved = staging[pl.ds(i, L, stride=Q), :].T
             gated = key[tokens, lanes].astype(F32) * value[tokens, lanes].astype(F32)
-            mixed[tokens, lanes] = (
+            mixed[level, tokens, lanes] = (
                 query[tokens, lanes].astype(F32) * (convolved + gain[:, lanes] * gated)
             ).astype(BF16)
+        ring_send(1, g)
 
     convolve(0)
 
     @pl.loop(1, G)
     def _(g):
         convolve(g)
+
+        @pl.when(g >= 2)
+        def _():
+            forward(2, g - 2)
+
         combine(g - 1)
 
+        @pl.when(g >= 2)
+        def _():
+            forward(3, g - 2)
+
+        @pl.when(g >= 3)
+        def _():
+            forward(4, g - 3)
+
+    weight_second()
     combine(G - 1)
+    forward(2, G - 2)
+    forward(4, G - 3)
+    forward(2, G - 1)
+    forward(3, G - 2)
+    weight_third()
+    forward(3, G - 1)
+    forward(4, G - 2)
+    forward(4, G - 1)
+    for g in range(G):
+        ring_arrive(Z // 2, g)
+    wait(weight.at[:, pl.ds(0, S // 2)], got_weight.at[4])
+
+    total = spectrum.at[0]
+    total[...] = jnp.zeros((T, T), F32)
+
+    @pl.loop(0, Z)
+    def _(z):
+        total[...] += dot(mixed[z], weight[z].reshape(T, T), 1, 0)
+
+    out[...] = total[...].astype(BF16)
     arrive(gated_out, sent_gated)
+    weight_sent()
     for g in range(G):
         arrive(filter_out.at[g], sent_filter.at[g])
         arrive(conv_out.at[g], sent_conv.at[g])
+        for hop in range(1, Z // 2 + 1):
+            for way in range(2):
+                wait(ring_part(way, hop, g, 0), sent_ring.at[way, hop - 1, g])
 
 
 def whole(count):
@@ -231,22 +374,12 @@
 
 def body(gate_query, gate_key, gate_value, skip_gain, filter_spectra, out_weight):
     tab = tables()
-    groups = lax.axis_size("ch")
-    rank = lax.axis_index("seq")
-    outputs = out_weight.shape[1] // groups
-
-    share = lax.dynamic_slice_in_dim(out_weight, rank * C, C, 0)
-    share = lax.all_to_all(
-        share.reshape(C, groups, outputs), "ch", split_axis=1, concat_axis=0, tiled=False
-    )
-    weight = lax.all_gather(share.reshape(groups, C, outputs), "seq", axis=0)
-    weight = jnp.transpose(weight, (1, 0, 2, 3)).reshape(groups * T, outputs)
-
+    spectra = filter_spectra.reshape(KL * R, 2, G, L).transpose(0, 2, 1, 3)
     dma = pltpu.SemaphoreType.DMA
-    mixed = pl.pallas_call(
-        seq_kernel,
+    return pl.pallas_call(
+        kernel,
         out_shape=jax.ShapeDtypeStruct((T, T), BF16),
-        in_specs=whole(5 + len(NAMES)),
+        in_specs=whole(5) + [pl.BlockSpec(memory_space=pl.ANY)] + whole(len(NAMES)),
         out_specs=whole(1)[0],
         scratch_shapes=[
             VMEM((S, C, T), BF16),
@@ -255,7 +388,10 @@
             VMEM((G, S, Q, KL, L), BF16),
             VMEM((G, S, C, L), BF16),
             VMEM((G, S, C, L), BF16),
-            VMEM((L * KL, L), F32),
+            VMEM((C, Z * T), BF16),
+            VMEM((Z, S, C, T), BF16),
+            VMEM((Z, T, T), BF16),
+            VMEM((G, L * KL, L), F32),
             VMEM((T, T), BF16),
             VMEM((T, 2 * T), BF16),
             VMEM((G, K, T), F32),
@@ -264,11 +400,18 @@
             VMEM((3 * T, T), BF16),
             VMEM((T, L), F32),
             dma(()),
+            dma(()),
             dma((G,)),
             dma((G,)),
             dma(()),
+            dma((5,)),
+            dma((2, Z // 2, G)),
+            dma(()),
             dma((G,)),
             dma((G,)),
+            dma(()),
+            dma((5,)),
+            dma((2, Z // 2, G)),
         ],
         compiler_params=pltpu.CompilerParams(
             collective_id=0, has_side_effects=True, vmem_limit_bytes=52 << 20
@@ -279,11 +422,10 @@
         gate_key,
         gate_value,
         skip_gain[None, :],
-        filter_spectra.reshape(KL * R * 2, T),
+        spectra.reshape(KL * R * G * 2, L),
+        out_weight,
         *(jnp.asarray(tab[name]) for name in NAMES),
     )
-    mixed = lax.all_gather(mixed, "ch", axis=1, tiled=True)
-    return jnp.dot(mixed, weight, preferred_element_type=F32).astype(BF16)
 
 
 def solution(mesh):

time: 160 us -> 106 us (0.66); the launches traced: 160 us -> 104 us
  waiting for transfers between devices: 55.3 us -> 0 us
  Pallas kernels: 57.8 us -> 97.9 us
  blocking collectives: 16.7 us -> 0 us
  between operations: 13.5 us -> 0.02 us
  matrix products: 6.59 us -> 0 us
  local copies, waits for them, and re-layouts: 10 us -> 6.27 us
    all_gather x2 -> x0, waiting for transfers between devices: 55.3 us -> none  [the longest x1 50.2 us: body(): mixed = lax.all_gather(mixed, 'ch', axis=1, tiled=True)]
    pallas_call x1, Pallas kernels: 57.8 us -> 97.9 us  [body(): pl.pallas_call(kernel, out_shape=jax.ShapeDtypeStruct((T, T), BF16), in_s...]
    all_to_all x1 -> x0, blocking collectives: 16.7 us -> none  [body(): lax.all_to_all(share.reshape(C, groups, outputs), 'ch', split_axis=1, con...]
    dot_general x1 -> x0, matrix products: 6.59 us -> none  [body(): return jnp.dot(mixed, weight, preferred_element_type=F32).astype(BF16)]
    unnamed x15 -> x13, local copies, waits for them, and re-layouts: 0.07 us -> 6.27 us
    transpose x1 -> x0, local copies, waits for them, and re-layouts: 4.77 us -> none  [body(): weight = jnp.transpose(weight, (1, 0, 2, 3)).reshape(groups * T, outputs)]
    reshape x1 -> x0, local copies, waits for them, and re-layouts: 4.11 us -> none  [body(): filter_spectra.reshape(KL * R * 2, T)]
  transfers between devices with their start and end apart: 2 -> 0, of which waited for: 2 -> 0; matrix products, arithmetic and copies ran while one was open for 6% -> 0% of each run, Pallas kernels for 36% -> 0%
where the time goes in v3:
time: 106 us; the launch traced here: 104 us
  Pallas kernels  97.9 us (92%)
  local copies, waits for them, and re-layouts  6.27 us (6%)
    pallas_call x1, Pallas kernels, body(): pl.pallas_call(kernel, out_shape=jax.ShapeDtypeStruct((T, T), BF16), in_s...  97.9 us
    unnamed x13, local copies, waits for them, and re-layouts  6.27 us

profile of v3, /device:TPU:1, one launch (start us, length us, event | category | flops | bytes accessed | tf_op | source)
XLA Modules:
  0.0 104.2 jit_solution(7608868073146443935)
XLA Ops:
  0.0 0.0 copy-start
  0.0 1.0 copy-done
  1.0 0.0 copy-start.1
  1.0 0.7 copy-done.1
  1.7 0.0 copy-start.2
  1.7 1.0 copy-done.2
  2.7 0.0 copy-start.3
  2.7 0.9 copy-done.3
  3.7 0.0 copy-start.4
  3.7 0.9 copy-done.4
  4.6 0.0 copy-start.5
  4.6 0.9 copy-done.5
  5.5 97.9 %shard_map.145 = bf16[512,512]{1,0:T(8,128)(2,1)S(1)} custom-call(bf16[512,512]{1,0:T(8,128)(2,1)S(1)} %copy-done, bf16[512,512]{1,0:T(8,128)(2,1)} %key.1, bf16[512,512]{1,0:T(8,128)(2,1)} %value.1, f32[1,512]{1,0:T(1,128)S(1)} %bitcast.6, bf16[8192,128]{1,0:T(8,128)(2,1)} %bitcast.7, bf16[512,4096]{1,0:T(8,128)(2,1)} %weight_here.1, ...), custom_call_target="tpu_custom_call" | custom-call | flops 12000000000 | bytes 8388608 | tf_op jit(solution)/shard_map/pallas_call | solution.py:379
  103.4 0.8 copy.18
Async XLA Ops:
  0.0 1.0 copy-start
  1.0 0.7 copy-start.1
  1.7 1.0 copy-start.2
  2.7 0.9 copy-start.3
  3.7 0.9 copy-start.4
  4.6 0.9 copy-start.5

commit v4 on v3

--- a/solution.py
+++ b/solution.py
@@ -52,29 +52,16 @@
         for g in range(G):
             for part in range(2):
                 order[(q * G + g) * 2 + part, (g * 2 + part) * R + q] = 1
-    spread = np.zeros((T, T), ml_dtypes.bfloat16)
-    gather = np.zeros((T, T), ml_dtypes.bfloat16)
-    for j in range(S):
-        for g in range(G):
-            for c in range(Q):
-                spread[j * C + g * Q + c, g * L + j * Q + c] = 1
-                gather[(g * Q + c) * S + j, j * C + g * Q + c] = 1
     return dict(
+        order=order,
         first=first,
-        turn_cos=np.cos(turn).astype(np.float32),
-        turn_sin=np.sin(turn).astype(np.float32),
-        inner_high=inner_high,
-        inner_low=inner_low,
+        turn=np.concatenate([np.cos(turn), np.sin(turn)], 0).astype(np.float32),
+        inner=np.stack([inner_high, inner_low]),
         last=last,
-        order=order,
-        spread=spread,
-        gather=gather,
     )
 
 
-NAMES = (
-    "first", "turn_cos", "turn_sin", "inner_high", "inner_low", "last", "order", "spread", "gather"
-)
+NAMES = ("order", "first", "turn", "inner", "last")
 
 
 def dot(left, right, left_dim, right_dim):
@@ -93,18 +80,23 @@
 
 
 def kernel(
-    query, key, value, gain, spectra, weight_here, first, turn_cos, turn_sin, inner_high, inner_low,
-    last, order, spread, gather, out, gated_out, gated_in, filter_out, filter_in, conv_out, conv_in,
-    share, weight, mixed, wide, sorted_in, rows, spectrum, product, back, turned, staging, local,
-    sent_gated, sent_filter, sent_conv, sent_share, sent_weight, sent_ring, got_gated, got_filter,
-    got_conv, got_share, got_weight, got_ring,
+    query_here, key_here, value_here, gain_here, spectra_here, weight_here, order_here, first_here,
+    turn_here, inner_here, last_here, out, query, key, value, gain, spectra, order, first, turn,
+    inner, last, gated_out, gated_in, filter_out, filter_in, conv_out, conv_in, share, weight, mixed,
+    wide, rows, spectrum, product, back, turned, staging, loaded, sent_gated, sent_filter, sent_conv,
+    sent_share, sent_weight, sent_ring, got_gated, got_filter, got_conv, got_share, got_weight,
+    got_ring,
 ):
     me, level = lax.axis_index("seq"), lax.axis_index("ch")
     core, x, y = lax.rem(me, 2), lax.rem(me // 2, 4), me // 8
     sibling = me + 1 - 2 * core
 
     def peer(k):
-        return lax.rem(me + k, S)
+        away_x = lax.rem(k, 4)
+        away_y = lax.rem(k // 4 + away_x, 4)
+        return (
+            lax.rem(y + away_y, 4) * 8 + lax.rem(x + away_x, 4) * 2 + lax.rem(core + k // 16, 2)
+        )
 
     def at_level(k):
         return lax.rem(level + k + Z, Z)
@@ -115,10 +107,6 @@
     def along_y(k):
         return lax.rem(y + k, 4) * 8 + x * 2 + core
 
-    share_load = pltpu.make_async_copy(
-        weight_here.at[pl.ds(pl.multiple_of(me * C, C), C), :], share, local
-    )
-    share_load.start()
     barrier = pltpu.get_barrier_semaphore()
 
     @pl.loop(1, S)
@@ -128,6 +116,20 @@
     @pl.loop(1, Z)
     def _(k):
         pl.semaphore_signal(barrier, inc=1, device_id={"ch": at_level(k)}, device_id_type=MESH)
+
+    share_here = weight_here.at[pl.ds(pl.multiple_of(me * C, C), C), :]
+    loads = [
+        pltpu.make_async_copy(source, target, loaded.at[i])
+        for i, (source, target) in enumerate(
+            (
+                (key_here, key), (value_here, value), (spectra_here, spectra), (order_here, order),
+                (share_here, share), (first_here, first), (turn_here, turn), (inner_here, inner),
+                (last_here, last), (query_here, query), (gain_here, gain),
+            )
+        )
+    ]
+    for load in loads:
+        load.start()
 
     def send(source, target, sent, got, **to):
         pltpu.make_async_remote_copy(
@@ -207,7 +209,8 @@
         tokens = pl.ds(0, T)
         if hop == Z // 2:
             tokens = pl.ds(way * (T // 2), T // 2)
-        return mixed.at[source, tokens, chunk_lanes(g)]
+        lanes = pl.ds(pl.multiple_of(source * T + g * L, L), L)
+        return mixed.at[tokens, lanes]
 
     def ring_send(hop, g):
         for way, sign in enumerate((1, -1)):
@@ -225,8 +228,12 @@
         ring_arrive(hop - 1, g)
         ring_send(hop, g)
 
-    def gated_values():
-        return key[...].astype(F32) * value[...].astype(F32)
+    def prepare_gated(g):
+        lanes = chunk_lanes(g)
+        gated = (key[:, lanes].astype(F32) * value[:, lanes].astype(F32)).T
+        for i in range(T // L):
+            staging[pl.ds(i, L, stride=Q), :] = gated[:, i * L : (i + 1) * L]
+        gated_out[g] = staging[...].astype(BF16).reshape(S, C, L)
 
     def prepare_filter():
         @pl.loop(0, KL)
@@ -236,64 +243,61 @@
             for g in range(G):
                 wide[g, pl.ds(k, L, stride=KL), :] = moved[:, g * L : (g + 1) * L]
 
-    gated_out[...] = (
-        dot(spread[...], gated_values().astype(BF16), 1, 1).astype(BF16).reshape(S, C, T)
-    )
-    pl.semaphore_wait(barrier, S + Z - 2)
-    send_all(gated_out, gated_in, sent_gated, got_gated)
-    share_load.wait()
-    spread_share()
-    prepare_filter()
-
-    @pl.loop(0, G)
-    def _(g):
-        filter_out[g] = wide[g].astype(BF16).reshape(S, Q, KL, L)
-        send_all(filter_out.at[g], filter_in.at[g], sent_filter.at[g], got_filter.at[g])
-
-    weight_first()
-    arrive(gated_in, got_gated)
-    sorted_in[...] = dot(gather[...], gated_in[...].reshape(T, T), 1, 0).astype(BF16)
-
-    @pl.loop(0, G)
-    def _(g):
-        values = sorted_in[pl.ds(pl.multiple_of(g * L, L), L), :]
-        back[:, :T] = dot(first[...], jnp.concatenate([values, values], 0), 1, 0)
+    def round_filter(g):
+        for h in range(2):
+            part = wide[g].astype(BF16).reshape(S, Q, KL, L)[:, h * Q // 2 : (h + 1) * Q // 2]
+            filter_out[g, h] = part
+
+    def transform(g):
+        staging[...] = gated_in[g].reshape(T, L).astype(F32)
+        for c in range(Q):
+            for i in range(T // L):
+                part = staging[pl.ds(c * Q + i, S, stride=C), :].astype(BF16)
+                for copy in range(2):
+                    at = copy * L + c * S
+                    turned[at : at + S, i * L : (i + 1) * L] = part
+        back[:, :T] = dot(first[...], turned[: 2 * L, :], 1, 0)
         for c in range(Q):
             at = c * 2 * R
             real, imag = back[at : at + R, :T], back[at + R : at + 2 * R, :T]
-            turned_real = (real * turn_cos[...] + imag * turn_sin[...]).astype(BF16)
-            turned_imag = (imag * turn_cos[...] - real * turn_sin[...]).astype(BF16)
+            turned_real = (real * turn[:R] + imag * turn[R:]).astype(BF16)
+            turned_imag = (imag * turn[:R] - real * turn[R:]).astype(BF16)
             rows[at : at + R, :T] = turned_real
             rows[at : at + R, T:] = turned_imag
             rows[at + R : at + 2 * R, :T] = turned_imag
             rows[at + R : at + 2 * R, T:] = -turned_real
-        spectrum[g] = dot(inner_high[...], rows[...], 1, 1) + dot(inner_low[...], rows[...], 1, 1)
-
-    def convolve(g):
-        arrive(filter_in.at[g], got_filter.at[g])
+        spectrum[g] = dot(inner[0], rows[...], 1, 1) + dot(inner[1], rows[...], 1, 1)
+
+    def multiply(g):
         is_real = lax.broadcasted_iota(jnp.int32, (K, L), 1) < R
         for c in range(Q):
             lanes = slice(c * L, (c + 1) * L)
-            response = filter_in[g, :, c].reshape(K, L).astype(F32)
+            response = filter_in[g, c // 2, :, c % 2].reshape(K, L).astype(F32)
             swapped = pltpu.roll(response, R, 1)
             value_c = spectrum[g, :, lanes]
             product[:, lanes] = (
                 value_c * jnp.where(is_real, response, swapped)
                 + pltpu.roll(value_c, R, 1) * jnp.where(is_real, -swapped, response)
             ).astype(BF16)
-        back[...] = dot(product[...], inner_high[...], 0, 0) + dot(product[...], inner_low[...], 0, 0)
+
+    def invert():
+        back[...] = dot(product[...], inner[0], 0, 0) + dot(product[...], inner[1], 0, 0)
+
+    def unturn():
         for c in range(Q):
             at = c * 2 * R
             real = back[at : at + R, :T] - back[at + R : at + 2 * R, T:]
             imag = back[at : at + R, T:] + back[at + R : at + 2 * R, :T]
             for at, part in (
-                (at, real * turn_cos[...] - imag * turn_sin[...]),
-                (at + R, real * turn_sin[...] + imag * turn_cos[...]),
+                (at, real * turn[:R] - imag * turn[R:]),
+                (at + R, real * turn[R:] + imag * turn[:R]),
             ):
                 high, low = split(part)
                 turned[at : at + R, :] = high
                 turned[T + at : T + at + R, :] = high
                 turned[2 * T + at : 2 * T + at + R, :] = low
+
+    def finish(g):
         result = dot(last[...], turned[...], 1, 0)
         for c in range(Q):
             for i in range(T // L):
@@ -301,75 +305,123 @@
                     c * S : (c + 1) * S, i * L : (i + 1) * L
                 ]
         conv_out[g] = staging[...].astype(BF16).reshape(S, C, L)
-        send_all(conv_out.at[g], conv_in.at[g], sent_conv.at[g], got_conv.at[g])
-
-    def combine(g):
-        arrive(conv_in.at[g], got_conv.at[g])
+
+    def mix(g):
         staging[...] = conv_in[g].reshape(T, L).astype(F32)
         lanes = chunk_lanes(g)
         for i in range(T // L):
             tokens = slice(i * L, (i + 1) * L)
             convolved = staging[pl.ds(i, L, stride=Q), :].T
             gated = key[tokens, lanes].astype(F32) * value[tokens, lanes].astype(F32)
-            mixed[level, tokens, lanes] = (
+            mixed[tokens, pl.ds(pl.multiple_of(level * T + g * L, L), L)] = (
                 query[tokens, lanes].astype(F32) * (convolved + gain[:, lanes] * gated)
             ).astype(BF16)
+
+    def project():
+        out[...] = dot(mixed[...], weight[...].reshape(Z * T, T), 1, 0).astype(BF16)
+
+    def send_gated(g):
+        send_all(gated_out.at[g], gated_in.at[g], sent_gated.at[g], got_gated.at[g])
+
+    def send_filter(g, h):
+        send_all(
+            filter_out.at[g, h], filter_in.at[g, h], sent_filter.at[g, h], got_filter.at[g, h]
+        )
+
+    def convolve(g):
+        arrive(filter_in.at[g, 0], got_filter.at[g, 0])
+        arrive(filter_in.at[g, 1], got_filter.at[g, 1])
+        multiply(g)
+        invert()
+        unturn()
+        finish(g)
+        send_all(conv_out.at[g], conv_in.at[g], sent_conv.at[g], got_conv.at[g])
+
+    def combine(g):
+        arrive(conv_in.at[g], got_conv.at[g])
+        mix(g)
         ring_send(1, g)
 
-    convolve(0)
-
-    @pl.loop(1, G)
+    for load in loads[:2]:
+        load.wait()
+
+    @pl.loop(0, G)
     def _(g):
+        prepare_gated(g)
+
+    for load in loads[2:4]:
+        load.wait()
+    prepare_filter()
+
+    @pl.loop(0, G)
+    def _(g):
+        round_filter(g)
+
+    for load in loads[4:]:
+        load.wait()
+    pl.semaphore_wait(barrier, S + Z - 2)
+    send_gated(0)
+    send_filter(0, 0)
+    send_filter(0, 1)
+    send_gated(1)
+    send_filter(1, 0)
+    spread_share()
+
+    @pl.loop(0, G)
+    def _(g):
+        arrive(gated_in.at[g], got_gated.at[g])
+        transform(g)
+
+        @pl.when(g >= 1)
+        def _():
+            forward(2, g - 1)
+
         convolve(g)
 
-        @pl.when(g >= 2)
-        def _():
-            forward(2, g - 2)
-
-        combine(g - 1)
-
-        @pl.when(g >= 2)
-        def _():
-            forward(3, g - 2)
-
-        @pl.when(g >= 3)
-        def _():
-            forward(4, g - 3)
-
-    weight_second()
-    combine(G - 1)
-    forward(2, G - 2)
-    forward(4, G - 3)
+        @pl.when(g < G - 1)
+        def _():
+            send_filter(g + 1, 1)
+
+        @pl.when(g < G - 2)
+        def _():
+            send_gated(g + 2)
+            send_filter(g + 2, 0)
+
+        @pl.when(g == 1)
+        def _():
+            weight_first()
+
+        @pl.when(g == G - 1)
+        def _():
+            weight_second()
+
+        @pl.when(g >= 1)
+        def _():
+            forward(3, g - 1)
+
+        combine(g)
+
+        @pl.when(g >= 1)
+        def _():
+            forward(4, g - 1)
+
     forward(2, G - 1)
-    forward(3, G - 2)
+    forward(3, G - 1)
     weight_third()
-    forward(3, G - 1)
-    forward(4, G - 2)
     forward(4, G - 1)
     for g in range(G):
         ring_arrive(Z // 2, g)
     wait(weight.at[:, pl.ds(0, S // 2)], got_weight.at[4])
-
-    total = spectrum.at[0]
-    total[...] = jnp.zeros((T, T), F32)
-
-    @pl.loop(0, Z)
-    def _(z):
-        total[...] += dot(mixed[z], weight[z].reshape(T, T), 1, 0)
-
-    out[...] = total[...].astype(BF16)
-    arrive(gated_out, sent_gated)
+    project()
     weight_sent()
     for g in range(G):
-        arrive(filter_out.at[g], sent_filter.at[g])
+        arrive(gated_out.at[g], sent_gated.at[g])
+        arrive(filter_out.at[g, 0], sent_filter.at[g, 0])
+        arrive(filter_out.at[g, 1], sent_filter.at[g, 1])
         arrive(conv_out.at[g], sent_conv.at[g])
         for hop in range(1, Z // 2 + 1):
             for way in range(2):
                 wait(ring_part(way, hop, g, 0), sent_ring.at[way, hop - 1, g])
-
-
-def whole(count):
-    return [pl.BlockSpec(memory_space=VMEM)] * count
 
 
 def body(gate_query, gate_key, gate_value, skip_gain, filter_spectra, out_weight):
@@ -379,42 +431,51 @@
     return pl.pallas_call(
         kernel,
         out_shape=jax.ShapeDtypeStruct((T, T), BF16),
-        in_specs=whole(5) + [pl.BlockSpec(memory_space=pl.ANY)] + whole(len(NAMES)),
-        out_specs=whole(1)[0],
+        in_specs=[pl.BlockSpec(memory_space=pltpu.HBM)] * (6 + len(NAMES)),
+        out_specs=pl.BlockSpec(memory_space=VMEM),
         scratch_shapes=[
-            VMEM((S, C, T), BF16),
-            VMEM((S, C, T), BF16),
-            VMEM((G, S, Q, KL, L), BF16),
-            VMEM((G, S, Q, KL, L), BF16),
+            VMEM((T, T), BF16),
+            VMEM((T, T), BF16),
+            VMEM((T, T), BF16),
+            VMEM((1, T), F32),
+            VMEM((KL * R * G * 2, L), BF16),
+            VMEM((2 * R * G, 2 * R * G), BF16),
+            VMEM((T, 2 * L), BF16),
+            VMEM((2 * R, T), F32),
+            VMEM((2, K, 2 * T), BF16),
+            VMEM((L, 3 * T), BF16),
+            VMEM((G, S, C, L), BF16),
+            VMEM((G, S, C, L), BF16),
+            VMEM((G, 2, S, Q // 2, KL, L), BF16),
+            VMEM((G, 2, S, Q // 2, KL, L), BF16),
             VMEM((G, S, C, L), BF16),
             VMEM((G, S, C, L), BF16),
             VMEM((C, Z * T), BF16),
             VMEM((Z, S, C, T), BF16),
-            VMEM((Z, T, T), BF16),
+            VMEM((T, Z * T), BF16),
             VMEM((G, L * KL, L), F32),
-            VMEM((T, T), BF16),
             VMEM((T, 2 * T), BF16),
             VMEM((G, K, T), F32),
             VMEM((K, T), BF16),
             VMEM((T, 2 * T), F32),
             VMEM((3 * T, T), BF16),
             VMEM((T, L), F32),
-            dma(()),
-            dma(()),
+            dma((11,)),
             dma((G,)),
+            dma((G, 2)),
             dma((G,)),
             dma(()),
             dma((5,)),
             dma((2, Z // 2, G)),
-            dma(()),
             dma((G,)),
+            dma((G, 2)),
             dma((G,)),
             dma(()),
             dma((5,)),
             dma((2, Z // 2, G)),
         ],
         compiler_params=pltpu.CompilerParams(
-            collective_id=0, has_side_effects=True, vmem_limit_bytes=52 << 20
+            collective_id=0, has_side_effects=True, vmem_limit_bytes=58 << 20
         ),
         cost_estimate=pl.CostEstimate(flops=12 * 10**9, bytes_accessed=8 << 20, transcendentals=0),
     )(

time: 106 us -> 102 us (0.962)
  the two profiles are of different devices: /device:TPU:1 before, /device:TPU:22 now
where the time goes in v4:
time: 102 us
  Pallas kernels  100 us (98%)
  local copies, waits for them, and re-layouts  1.87 us (2%)
    pallas_call x1, Pallas kernels, body(): pl.pallas_call(kernel, out_shape=jax.ShapeDtypeStruct((T, T), BF16), in_s...  100 us

profile of v4, /device:TPU:22, one launch (start us, length us, event | category | flops | bytes accessed | tf_op | source)
XLA Modules:
  0.0 101.9 jit_solution(8601000403565334394)
XLA Ops:
  0.0 100.0 %shard_map.109 = bf16[512,512]{1,0:T(8,128)(2,1)} custom-call(bf16[512,512]{1,0:T(8,128)(2,1)} %query_here.1, bf16[512,512]{1,0:T(8,128)(2,1)} %key_here.1, bf16[512,512]{1,0:T(8,128)(2,1)} %value_here.1, f32[1,512]{1,0:T(1,128)} %bitcast.7, bf16[8192,128]{1,0:T(8,128)(2,1)} %bitcast.6, bf16[512,4096]{1,0:T(8,128)(2,1)} %weight_here.1, ...), custom_call_target="tpu_custom_call" | custom-call | flops 12000000000 | bytes 8388608 | tf_op jit(solution)/shard_map/pallas_call | solution.py:431
  100.0 1.9 %copy.14 = bf16[512,512]{1,0:T(8,128)(2,1)} copy(bf16[512,512]{1,0:T(8,128)(2,1)} %shard_map.109) | data formatting | bytes 1048576

commit v5 on v4

--- a/solution.py
+++ b/solution.py
@@ -75,8 +75,12 @@
     return high, (values - high.astype(F32)).astype(BF16)
 
 
+def lanes_at(start, size=L):
+    return pl.ds(start if isinstance(start, int) else pl.multiple_of(start, L), size)
+
+
 def chunk_lanes(g):
-    return pl.ds(pl.multiple_of(g * L, L), L)
+    return lanes_at(g * L)
 
 
 def kernel(
@@ -151,7 +155,7 @@
         wait(target.at[pl.ds(0, S - 1)], sem)
 
     def share_lanes(k):
-        return pl.ds(pl.multiple_of(k * T, T), T)
+        return lanes_at(k * T, T)
 
     def spread_share():
         @pl.loop(1, Z)
@@ -209,7 +213,7 @@
         tokens = pl.ds(0, T)
         if hop == Z // 2:
             tokens = pl.ds(way * (T // 2), T // 2)
-        lanes = pl.ds(pl.multiple_of(source * T + g * L, L), L)
+        lanes = lanes_at(source * T + g * L)
         return mixed.at[tokens, lanes]
 
     def ring_send(hop, g):
@@ -244,9 +248,7 @@
                 wide[g, pl.ds(k, L, stride=KL), :] = moved[:, g * L : (g + 1) * L]
 
     def round_filter(g):
-        for h in range(2):
-            part = wide[g].astype(BF16).reshape(S, Q, KL, L)[:, h * Q // 2 : (h + 1) * Q // 2]
-            filter_out[g, h] = part
+        filter_out[g] = wide[g].astype(BF16).reshape(S, Q, KL, L)
 
     def transform(g):
         staging[...] = gated_in[g].reshape(T, L).astype(F32)
@@ -272,7 +274,7 @@
         is_real = lax.broadcasted_iota(jnp.int32, (K, L), 1) < R
         for c in range(Q):
             lanes = slice(c * L, (c + 1) * L)
-            response = filter_in[g, c // 2, :, c % 2].reshape(K, L).astype(F32)
+            response = filter_in[g, :, c].reshape(K, L).astype(F32)
             swapped = pltpu.roll(response, R, 1)
             value_c = spectrum[g, :, lanes]
             product[:, lanes] = (
@@ -313,24 +315,31 @@
             tokens = slice(i * L, (i + 1) * L)
             convolved = staging[pl.ds(i, L, stride=Q), :].T
             gated = key[tokens, lanes].astype(F32) * value[tokens, lanes].astype(F32)
-            mixed[tokens, pl.ds(pl.multiple_of(level * T + g * L, L), L)] = (
+            mixed[tokens, lanes_at(level * T + g * L)] = (
                 query[tokens, lanes].astype(F32) * (convolved + gain[:, lanes] * gated)
             ).astype(BF16)
 
-    def project():
-        out[...] = dot(mixed[...], weight[...].reshape(Z * T, T), 1, 0).astype(BF16)
+    def project(source):
+        return dot(mixed[:, share_lanes(source)], weight[source].reshape(T, T), 1, 0)
+
+    def project_near():
+        total = spectrum.at[0]
+        total[...] = project(level)
+        for k in (1, -1, 2, -2):
+            total[...] += project(at_level(k))
+
+    def project_far():
+        total = spectrum[0] + project(at_level(3)) + project(at_level(-3))
+        out[...] = (total + project(at_level(4))).astype(BF16)
 
     def send_gated(g):
         send_all(gated_out.at[g], gated_in.at[g], sent_gated.at[g], got_gated.at[g])
 
-    def send_filter(g, h):
-        send_all(
-            filter_out.at[g, h], filter_in.at[g, h], sent_filter.at[g, h], got_filter.at[g, h]
-        )
+    def send_filter(g):
+        send_all(filter_out.at[g], filter_in.at[g], sent_filter.at[g], got_filter.at[g])
 
     def convolve(g):
-        arrive(filter_in.at[g, 0], got_filter.at[g, 0])
-        arrive(filter_in.at[g, 1], got_filter.at[g, 1])
+        arrive(filter_in.at[g], got_filter.at[g])
         multiply(g)
         invert()
         unturn()
@@ -342,6 +351,14 @@
         mix(g)
         ring_send(1, g)
 
+    def begin(g):
+        arrive(gated_in.at[g], got_gated.at[g])
+        transform(g)
+
+    def follow(g):
+        send_gated(g)
+        send_filter(g)
+
     for load in loads[:2]:
         load.wait()
 
@@ -352,72 +369,55 @@
     for load in loads[2:4]:
         load.wait()
     prepare_filter()
-
-    @pl.loop(0, G)
-    def _(g):
-        round_filter(g)
-
+    round_filter(0)
+    pl.semaphore_wait(barrier, S + Z - 2)
+    follow(0)
+    round_filter(1)
+    follow(1)
     for load in loads[4:]:
         load.wait()
-    pl.semaphore_wait(barrier, S + Z - 2)
-    send_gated(0)
-    send_filter(0, 0)
-    send_filter(0, 1)
-    send_gated(1)
-    send_filter(1, 0)
     spread_share()
-
-    @pl.loop(0, G)
-    def _(g):
-        arrive(gated_in.at[g], got_gated.at[g])
-        transform(g)
-
-        @pl.when(g >= 1)
-        def _():
-            forward(2, g - 1)
-
-        convolve(g)
-
-        @pl.when(g < G - 1)
-        def _():
-            send_filter(g + 1, 1)
-
-        @pl.when(g < G - 2)
-        def _():
-            send_gated(g + 2)
-            send_filter(g + 2, 0)
-
-        @pl.when(g == 1)
-        def _():
-            weight_first()
-
-        @pl.when(g == G - 1)
-        def _():
-            weight_second()
-
-        @pl.when(g >= 1)
-        def _():
-            forward(3, g - 1)
-
-        combine(g)
-
-        @pl.when(g >= 1)
-        def _():
-            forward(4, g - 1)
-
-    forward(2, G - 1)
-    forward(3, G - 1)
+    round_filter(2)
+    round_filter(3)
+
+    begin(0)
+    convolve(0)
+    follow(2)
+    begin(1)
+    convolve(1)
+    combine(0)
+    follow(3)
+    begin(2)
+    convolve(2)
+    forward(2, 0)
+    combine(1)
+    weight_first()
+    begin(3)
+    forward(3, 0)
+    convolve(3)
+    forward(2, 1)
+    combine(2)
+    forward(4, 0)
+    weight_second()
+    forward(3, 1)
+    forward(2, 2)
+    combine(3)
+    forward(4, 1)
+    forward(3, 2)
+    forward(2, 3)
+    forward(4, 2)
+    forward(3, 3)
     weight_third()
-    forward(4, G - 1)
+    forward(4, 3)
+    wait(weight.at[:, pl.ds(0, S // 2)], got_weight.at[4])
+    project_near()
     for g in range(G):
         ring_arrive(Z // 2, g)
-    wait(weight.at[:, pl.ds(0, S // 2)], got_weight.at[4])
-    project()
+    project_far()
     weight_sent()
     for g in range(G):
         arrive(gated_out.at[g], sent_gated.at[g])
-        arrive(filter_out.at[g, 0], sent_filter.at[g, 0])
-        arrive(filter_out.at[g, 1], sent_filter.at[g, 1])
+        arrive(filter_out.at[g], sent_filter.at[g])
         arrive(conv_out.at[g], sent_conv.at[g])
         for hop in range(1, Z // 2 + 1):
             for way in range(2):
@@ -446,8 +446,8 @@
             VMEM((L, 3 * T), BF16),
             VMEM((G, S, C, L), BF16),
             VMEM((G, S, C, L), BF16),
-            VMEM((G, 2, S, Q // 2, KL, L), BF16),
-            VMEM((G, 2, S, Q // 2, KL, L), BF16),
+            VMEM((G, S, Q, KL, L), BF16),
+            VMEM((G, S, Q, KL, L), BF16),
             VMEM((G, S, C, L), BF16),
             VMEM((G, S, C, L), BF16),
             VMEM((C, Z * T), BF16),
@@ -462,13 +462,13 @@
             VMEM((T, L), F32),
             dma((11,)),
             dma((G,)),
-            dma((G, 2)),
+            dma((G,)),
             dma((G,)),
             dma(()),
             dma((5,)),
             dma((2, Z // 2, G)),
             dma((G,)),
-            dma((G, 2)),
+            dma((G,)),
             dma((G,)),
             dma(()),
             dma((5,)),

time: 102 us -> 93.1 us (0.913)
  the two profiles are of different devices: /device:TPU:22 before, /device:TPU:1 now
where the time goes in v5:
time: 93.1 us; the launch traced here: 93 us
  Pallas kernels  91.1 us (98%)
  local copies, waits for them, and re-layouts  1.87 us (2%)
    pallas_call x1, Pallas kernels, body(): pl.pallas_call(kernel, out_shape=jax.ShapeDtypeStruct((T, T), BF16), in_s...  91.1 us
    unnamed x1, local copies, waits for them, and re-layouts  1.87 us

profile of v5, /device:TPU:1, one launch (start us, length us, event | category | flops | bytes accessed | tf_op | source)
XLA Modules:
  0.0 93.0 jit_solution(13417896093654859579)
XLA Ops:
  0.0 91.1 %shard_map.109 = bf16[512,512]{1,0:T(8,128)(2,1)} custom-call(bf16[512,512]{1,0:T(8,128)(2,1)} %query_here.1, bf16[512,512]{1,0:T(8,128)(2,1)} %key_here.1, bf16[512,512]{1,0:T(8,128)(2,1)} %value_here.1, f32[1,512]{1,0:T(1,128)} %bitcast.7, bf16[8192,128]{1,0:T(8,128)(2,1)} %bitcast.6, bf16[512,4096]{1,0:T(8,128)(2,1)} %weight_here.1, ...), custom_call_target="tpu_custom_call" | custom-call | flops 12000000000 | bytes 8388608 | tf_op jit(solution)/shard_map/pallas_call | solution.py:431
  91.1 1.9 %copy.14 = bf16[512,512]{1,0:T(8,128)(2,1)} copy(bf16[512,512]{1,0:T(8,128)(2,1)} %shard_map.109) | data formatting | bytes 1048576

commit v6 on v5

--- a/solution.py
+++ b/solution.py
@@ -328,9 +328,13 @@
         for k in (1, -1, 2, -2):
             total[...] += project(at_level(k))
 
-    def project_far():
-        total = spectrum[0] + project(at_level(3)) + project(at_level(-3))
-        out[...] = (total + project(at_level(4))).astype(BF16)
+    def project_next():
+        total = spectrum.at[0]
+        for k in (3, -3):
+            total[...] += project(at_level(k))
+
+    def project_last():
+        out[...] = (spectrum[0] + project(at_level(4))).astype(BF16)
 
     def send_gated(g):
         send_all(gated_out.at[g], gated_in.at[g], sent_gated.at[g], got_gated.at[g])
@@ -388,32 +392,33 @@
     combine(0)
     follow(3)
     begin(2)
-    convolve(2)
     forward(2, 0)
     combine(1)
+    convolve(2)
     weight_first()
+    forward(3, 0)
     begin(3)
-    forward(3, 0)
+    forward(2, 1)
     convolve(3)
-    forward(2, 1)
     combine(2)
+    forward(3, 1)
+    weight_second()
     forward(4, 0)
-    weight_second()
-    forward(3, 1)
-    forward(2, 2)
     combine(3)
     forward(4, 1)
+    forward(2, 2)
+    forward(2, 3)
     forward(3, 2)
-    forward(2, 3)
+    weight_third()
+    forward(3, 3)
     forward(4, 2)
-    forward(3, 3)
-    weight_third()
-    forward(4, 3)
     wait(weight.at[:, pl.ds(0, S // 2)], got_weight.at[4])
     project_near()
+    forward(4, 3)
+    project_next()
     for g in range(G):
         ring_arrive(Z // 2, g)
-    project_far()
+    project_last()
     weight_sent()
     for g in range(G):
         arrive(gated_out.at[g], sent_gated.at[g])
@@ -475,7 +480,7 @@
             dma((2, Z // 2, G)),
         ],
         compiler_params=pltpu.CompilerParams(
-            collective_id=0, has_side_effects=True, vmem_limit_bytes=58 << 20
+            collective_id=0, has_side_effects=True, vmem_limit_bytes=48 << 20
         ),
         cost_estimate=pl.CostEstimate(flops=12 * 10**9, bytes_accessed=8 << 20, transcendentals=0),
     )(

time: 93.1 us -> 94 us (level)
  local copies, waits for them, and re-layouts: 1.87 us -> 10.1 us
  Pallas kernels: 91.1 us -> 83.4 us
    unnamed x1 -> x19, local copies, waits for them, and re-layouts: 1.87 us -> 10.1 us
    pallas_call x1, Pallas kernels: 91.1 us -> 83.4 us  [body(): pl.pallas_call(kernel, out_shape=jax.ShapeDtypeStruct((T, T), BF16), in_s...]
where the time goes in v6:
time: 94 us; the launch traced here: 93.6 us
  Pallas kernels  83.4 us (89%)
  local copies, waits for them, and re-layouts  10.1 us (11%)
    pallas_call x1, Pallas kernels, body(): pl.pallas_call(kernel, out_shape=jax.ShapeDtypeStruct((T, T), BF16), in_s...  83.4 us
    unnamed x19, local copies, waits for them, and re-layouts  10.1 us

profile of v6, /device:TPU:1, one launch (start us, length us, event | category | flops | bytes accessed | tf_op | source)
XLA Modules:
  0.0 93.6 jit_solution(9426832198272404528)
XLA Ops:
  0.0 0.0 copy-start
  0.0 1.6 %copy-done = bf16[1024,2,512]{2,1,0:T(2,128)(2,1)S(1)} copy-done((bf16[1024,2,512]{2,1,0:T(2,128)(2,1)S(1)}, bf16[1024,2,512]{2,1,0:T(2,128)(2,1)}, u32[]{:S(2)}) %copy-start) | copy-done | bytes 2097176
  1.6 0.0 copy-start.1
  1.6 1.0 %copy-done.1 = bf16[512,512]{1,0:T(8,128)(2,1)S(1)} copy-done((bf16[512,512]{1,0:T(8,128)(2,1)S(1)}, bf16[512,512]{1,0:T(8,128)(2,1)}, u32[]{:S(2)}) %copy-start.1) | copy-done | bytes 524312
  2.6 0.0 copy-start.2
  2.6 1.0 %copy-done.2 = bf16[512,512]{1,0:T(8,128)(2,1)S(1)} copy-done((bf16[512,512]{1,0:T(8,128)(2,1)S(1)}, bf16[512,512]{1,0:T(8,128)(2,1)}, u32[]{:S(2)}) %copy-start.2) | copy-done | bytes 524312
  3.7 0.0 copy-start.3
  3.7 1.0 %copy-done.3 = bf16[512,512]{1,0:T(8,128)(2,1)S(1)} copy-done((bf16[512,512]{1,0:T(8,128)(2,1)S(1)}, bf16[512,512]{1,0:T(8,128)(2,1)}, u32[]{:S(2)}) %copy-start.3) | copy-done | bytes 524312
  4.7 0.0 copy-start.4
  4.7 0.7 copy-done.4
  5.4 0.0 copy-start.5
  5.4 1.0 %copy-done.5 = bf16[512,512]{1,0:T(8,128)(2,1)S(1)} copy-done((bf16[512,512]{1,0:T(8,128)(2,1)S(1)}, bf16[512,512]{1,0:T(8,128)(2,1)}, u32[]{:S(2)}) %copy-start.5) | copy-done | bytes 524312
  6.4 0.0 copy-start.6
  6.4 1.0 %copy-done.6 = bf16[128,1536]{1,0:T(8,128)(2,1)S(1)} copy-done((bf16[128,1536]{1,0:T(8,128)(2,1)S(1)}, bf16[128,1536]{1,0:T(8,128)(2,1)}, u32[]{:S(2)}) %copy-start.6) | copy-done | bytes 393240
  7.4 0.0 copy-start.7
  7.4 0.9 %copy-done.7 = f32[128,512]{1,0:T(8,128)S(1)} copy-done((f32[128,512]{1,0:T(8,128)S(1)}, f32[128,512]{1,0:T(8,128)}, u32[]{:S(2)}) %copy-start.7) | copy-done | bytes 262168
  8.4 0.0 copy-start.8
  8.4 0.9 %copy-done.8 = bf16[512,256]{1,0:T(8,128)(2,1)S(1)} copy-done((bf16[512,256]{1,0:T(8,128)(2,1)S(1)}, bf16[512,256]{1,0:T(8,128)(2,1)}, u32[]{:S(2)}) %copy-start.8) | copy-done | bytes 262168
  9.3 83.4 %shard_map.109 = bf16[512,512]{1,0:T(8,128)(2,1)S(1)} custom-call(bf16[512,512]{1,0:T(8,128)(2,1)S(1)} %copy-done.1, bf16[512,512]{1,0:T(8,128)(2,1)S(1)} %copy-done.2, bf16[512,512]{1,0:T(8,128)(2,1)S(1)} %copy-done.3, f32[1,512]{1,0:T(1,128)S(1)} %bitcast.7, bf16[8192,128]{1,0:T(8,128)(2,1)S(1)} %bitcast.6, bf16[512,4096]{1,0:T(8,128)(2,1)} %weight_here.1, ...), custom_call_target="tpu_custom_call" | custom-call | flops 12000000000 | bytes 8388608 | tf_op jit(solution)/shard_map/pallas_call | solution.py:436
  92.8 0.8 copy.14
Async XLA Ops:
  0.0 1.6 %copy-start = (bf16[1024,2,512]{2,1,0:T(2,128)(2,1)S(1)}, bf16[1024,2,512]{2,1,0:T(2,128)(2,1)}, u32[]{:S(2)}) copy-start(bf16[1024,2,512]{2,1,0:T(2,128)(2,1)} %param.15) | copy-start | bytes 6291460
  1.6 1.0 %copy-start.1 = (bf16[512,512]{1,0:T(8,128)(2,1)S(1)}, bf16[512,512]{1,0:T(8,128)(2,1)}, u32[]{:S(2)}) copy-start(bf16[512,512]{1,0:T(8,128)(2,1)} %query_here.1) | copy-start | bytes 1572868
  2.6 1.0 %copy-start.2 = (bf16[512,512]{1,0:T(8,128)(2,1)S(1)}, bf16[512,512]{1,0:T(8,128)(2,1)}, u32[]{:S(2)}) copy-start(bf16[512,512]{1,0:T(8,128)(2,1)} %key_here.1) | copy-start | bytes 1572868
  3.7 1.0 %copy-start.3 = (bf16[512,512]{1,0:T(8,128)(2,1)S(1)}, bf16[512,512]{1,0:T(8,128)(2,1)}, u32[]{:S(2)}) copy-start(bf16[512,512]{1,0:T(8,128)(2,1)} %value_here.1) | copy-start | bytes 1572868
  4.7 0.7 copy-start.4
  5.4 1.0 %copy-start.5 = (bf16[512,512]{1,0:T(8,128)(2,1)S(1)}, bf16[512,512]{1,0:T(8,128)(2,1)}, u32[]{:S(2)}) copy-start(bf16[512,512]{1,0:T(8,128)(2,1)} %constant.10.clone.order_here) | copy-start | bytes 1572868
  6.4 1.0 %copy-start.6 = (bf16[128,1536]{1,0:T(8,128)(2,1)S(1)}, bf16[128,1536]{1,0:T(8,128)(2,1)}, u32[]{:S(2)}) copy-start(bf16[128,1536]{1,0:T(8,128)(2,1)} %constant.14.clone.last_here) | copy-start | bytes 1179652
  7.4 0.9 %copy-start.7 = (f32[128,512]{1,0:T(8,128)S(1)}, f32[128,512]{1,0:T(8,128)}, u32[]{:S(2)}) copy-start(f32[128,512]{1,0:T(8,128)} %constant.12.clone.turn_here) | copy-start | bytes 786436
  8.4 0.9 %copy-start.8 = (bf16[512,256]{1,0:T(8,128)(2,1)S(1)}, bf16[512,256]{1,0:T(8,128)(2,1)}, u32[]{:S(2)}) copy-start(bf16[512,256]{1,0:T(8,128)(2,1)} %constant.11.clone.first_here) | copy-start | bytes 786436

commit v7 on v6

--- a/solution.py
+++ b/solution.py
@@ -480,7 +480,7 @@
             dma((2, Z // 2, G)),
         ],
         compiler_params=pltpu.CompilerParams(
-            collective_id=0, has_side_effects=True, vmem_limit_bytes=48 << 20
+            collective_id=0, has_side_effects=True, vmem_limit_bytes=58 << 20
         ),
         cost_estimate=pl.CostEstimate(flops=12 * 10**9, bytes_accessed=8 << 20, transcendentals=0),
     )(

time: 94 us -> 87.2 us (0.928)
  local copies, waits for them, and re-layouts: 10.1 us -> 1.87 us
  Pallas kernels: 83.4 us -> 85.2 us
    unnamed x19 -> x1, local copies, waits for them, and re-layouts: 10.1 us -> 1.87 us
    pallas_call x1, Pallas kernels: 83.4 us -> 85.2 us  [body(): pl.pallas_call(kernel, out_shape=jax.ShapeDtypeStruct((T, T), BF16), in_s...]
where the time goes in v7:
time: 87.2 us; the launch traced here: 87.1 us
  Pallas kernels  85.2 us (98%)
  local copies, waits for them, and re-layouts  1.87 us (2%)
    pallas_call x1, Pallas kernels, body(): pl.pallas_call(kernel, out_shape=jax.ShapeDtypeStruct((T, T), BF16), in_s...  85.2 us
    unnamed x1, local copies, waits for them, and re-layouts  1.87 us

profile of v7, /device:TPU:1, one launch (start us, length us, event | category | flops | bytes accessed | tf_op | source)
XLA Modules:
  0.0 87.1 jit_solution(8040606923515848430)
XLA Ops:
  0.0 85.2 %shard_map.109 = bf16[512,512]{1,0:T(8,128)(2,1)} custom-call(bf16[512,512]{1,0:T(8,128)(2,1)} %query_here.1, bf16[512,512]{1,0:T(8,128)(2,1)} %key_here.1, bf16[512,512]{1,0:T(8,128)(2,1)} %value_here.1, f32[1,512]{1,0:T(1,128)} %bitcast.7, bf16[8192,128]{1,0:T(8,128)(2,1)} %bitcast.6, bf16[512,4096]{1,0:T(8,128)(2,1)} %weight_here.1, ...), custom_call_target="tpu_custom_call" | custom-call | flops 12000000000 | bytes 8388608 | tf_op jit(solution)/shard_map/pallas_call | solution.py:436
  85.2 1.9 %copy.14 = bf16[512,512]{1,0:T(8,128)(2,1)} copy(bf16[512,512]{1,0:T(8,128)(2,1)} %shard_map.109) | data formatting | bytes 1048576

commit v8 on v7

--- a/solution.py
+++ b/solution.py
@@ -209,28 +209,31 @@
         wait(weight.at[upper, pl.ds(0, 12)], sent_weight.at[3])
         wait(weight.at[:, pl.ds(0, S // 2)], sent_weight.at[4])
 
-    def ring_part(way, hop, g, source):
-        tokens = pl.ds(0, T)
-        if hop == Z // 2:
-            tokens = pl.ds(way * (T // 2), T // 2)
-        lanes = lanes_at(source * T + g * L)
-        return mixed.at[tokens, lanes]
-
-    def ring_send(hop, g):
-        for way, sign in enumerate((1, -1)):
-            part = ring_part(way, hop, g, at_level(-sign * (hop - 1)))
-            send(
-                part, part, sent_ring.at[way, hop - 1, g], got_ring.at[way, hop - 1, g],
-                ch=at_level(sign),
-            )
-
-    def ring_arrive(hop, g):
-        for way, sign in enumerate((1, -1)):
-            wait(ring_part(way, hop, g, at_level(-sign * hop)), got_ring.at[way, hop - 1, g])
+    def ring_parts(way, hop):
+        return (way,) if hop == Z // 2 else (0, 1)
+
+    def ring_part(part, g, source):
+        return mixed.at[pl.ds(part * (T // 2), T // 2), lanes_at(source * T + g * L)]
+
+    def ring_send(way, hop, g, part):
+        sign = 1 - 2 * way
+        piece = ring_part(part, g, at_level(-sign * (hop - 1)))
+        send(
+            piece, piece, sent_ring.at[way, hop - 1, g, part], got_ring.at[way, hop - 1, g, part],
+            ch=at_level(sign),
+        )
+
+    def ring_arrive(way, hop, g, part):
+        sign = 1 - 2 * way
+        wait(ring_part(part, g, at_level(-sign * hop)), got_ring.at[way, hop - 1, g, part])
 
     def forward(hop, g):
-        ring_arrive(hop - 1, g)
-        ring_send(hop, g)
+        for part in range(2):
+            for way in range(2):
+                if part in ring_parts(way, hop - 1):
+                    ring_arrive(way, hop - 1, g, part)
+                if part in ring_parts(way, hop):
+                    ring_send(way, hop, g, part)
 
     def prepare_gated(g):
         lanes = chunk_lanes(g)
@@ -353,7 +356,9 @@
     def combine(g):
         arrive(conv_in.at[g], got_conv.at[g])
         mix(g)
-        ring_send(1, g)
+        for part in range(2):
+            for way in range(2):
+                ring_send(way, 1, g, part)
 
     def begin(g):
         arrive(gated_in.at[g], got_gated.at[g])
@@ -388,8 +393,8 @@
     convolve(0)
     follow(2)
     begin(1)
+    combine(0)
     convolve(1)
-    combine(0)
     follow(3)
     begin(2)
     forward(2, 0)
@@ -417,7 +422,8 @@
     forward(4, 3)
     project_next()
     for g in range(G):
-        ring_arrive(Z // 2, g)
+        for way in range(2):
+            ring_arrive(way, Z // 2, g, way)
     project_last()
     weight_sent()
     for g in range(G):
@@ -426,7 +432,8 @@
         arrive(conv_out.at[g], sent_conv.at[g])
         for hop in range(1, Z // 2 + 1):
             for way in range(2):
-                wait(ring_part(way, hop, g, 0), sent_ring.at[way, hop - 1, g])
+                for part in ring_parts(way, hop):
+                    wait(ring_part(part, g, 0), sent_ring.at[way, hop - 1, g, part])
 
 
 def body(gate_query, gate_key, gate_value, skip_gain, filter_spectra, out_weight):
@@ -471,13 +478,13 @@
             dma((G,)),
             dma(()),
             dma((5,)),
-            dma((2, Z // 2, G)),
+            dma((2, Z // 2, G, 2)),
             dma((G,)),
             dma((G,)),
             dma((G,)),
             dma(()),
             dma((5,)),
-            dma((2, Z // 2, G)),
+            dma((2, Z // 2, G, 2)),
         ],
         compiler_params=pltpu.CompilerParams(
             collective_id=0, has_side_effects=True, vmem_limit_bytes=58 << 20

time: 87.2 us -> 86.5 us (level)
  no operation moved by 1% of the time
where the time goes in v8:
time: 86.5 us; the launch traced here: 86.4 us
  Pallas kernels  84.5 us (98%)
  local copies, waits for them, and re-layouts  1.87 us (2%)
    pallas_call x1, Pallas kernels, body(): pl.pallas_call(kernel, out_shape=jax.ShapeDtypeStruct((T, T), BF16), in_s...  84.5 us
    unnamed x1, local copies, waits for them, and re-layouts  1.87 us

profile of v8, /device:TPU:1, one launch (start us, length us, event | category | flops | bytes accessed | tf_op | source)
XLA Modules:
  0.0 86.4 jit_solution(16850167993637106526)
XLA Ops:
  0.0 84.5 %shard_map.109 = bf16[512,512]{1,0:T(8,128)(2,1)} custom-call(bf16[512,512]{1,0:T(8,128)(2,1)} %query_here.1, bf16[512,512]{1,0:T(8,128)(2,1)} %key_here.1, bf16[512,512]{1,0:T(8,128)(2,1)} %value_here.1, f32[1,512]{1,0:T(1,128)} %bitcast.7, bf16[8192,128]{1,0:T(8,128)(2,1)} %bitcast.6, bf16[512,4096]{1,0:T(8,128)(2,1)} %weight_here.1, ...), custom_call_target="tpu_custom_call" | custom-call | flops 12000000000 | bytes 8388608 | tf_op jit(solution)/shard_map/pallas_call | solution.py:443
  84.6 1.9 %copy.14 = bf16[512,512]{1,0:T(8,128)(2,1)} copy(bf16[512,512]{1,0:T(8,128)(2,1)} %shard_map.109) | data formatting | bytes 1048576

commit v9 on v8

--- a/solution.py
+++ b/solution.py
@@ -20,6 +20,12 @@
 L = 128
 KL = K // S
 N = R * K
+AWAY = (
+    (2, 2), (1, 2), (2, 1), (3, 2), (2, 3), (2, 0), (0, 2), (1, 1), (3, 3), (1, 3), (3, 1), (1, 0),
+    (0, 1), (3, 0), (0, 3),
+)
+AWAY_X = sum(away[0] * 4**i for i, away in enumerate(AWAY))
+AWAY_Y = sum(away[1] * 4**i for i, away in enumerate(AWAY))
 MESH = pl.DeviceIdType.MESH
 VMEM = pltpu.VMEM
 BF16, F32 = jnp.bfloat16, jnp.float32
@@ -142,10 +148,17 @@
         ).start()
 
     def send_all(source, target, sent, got):
-        @pl.loop(1, S)
-        def _(k):
-            send(source.at[peer(k)], target.at[me], sent, got, seq=peer(k))
-
+        def step(_, away):
+            away_x, away_y = away
+            chip = (
+                lax.rem(y + lax.rem(away_y, 4), 4) * 8 + lax.rem(x + lax.rem(away_x, 4), 4) * 2
+            )
+            for c in range(2):
+                send(source.at[chip + c], target.at[me], sent, got, seq=chip + c)
+            return lax.div(away_x, 4), lax.div(away_y, 4)
+
+        lax.fori_loop(0, len(AWAY), step, (jnp.int32(AWAY_X), jnp.int32(AWAY_Y)))
+        send(source.at[sibling], target.at[me], sent, got, seq=sibling)
         target[me] = source[me]
 
     def wait(ref, sem):
@@ -396,22 +409,22 @@
     combine(0)
     convolve(1)
     follow(3)
+    forward(2, 0)
     begin(2)
-    forward(2, 0)
     combine(1)
+    forward(3, 0)
     convolve(2)
     weight_first()
-    forward(3, 0)
     begin(3)
     forward(2, 1)
     convolve(3)
     combine(2)
+    forward(4, 0)
     forward(3, 1)
     weight_second()
-    forward(4, 0)
     combine(3)
+    forward(2, 2)
     forward(4, 1)
-    forward(2, 2)
     forward(2, 3)
     forward(3, 2)
     weight_third()

time: 86.5 us -> 90.8 us (1.050)
  Pallas kernels: 84.5 us -> 88 us
    pallas_call x1, Pallas kernels: 84.5 us -> 88 us  [body(): pl.pallas_call(kernel, out_shape=jax.ShapeDtypeStruct((T, T), BF16), in_s...]
where the time goes in v9:
time: 90.8 us; the launch traced here: 89.9 us
  Pallas kernels  88 us (97%)
  local copies, waits for them, and re-layouts  1.87 us (2%)
    pallas_call x1, Pallas kernels, body(): pl.pallas_call(kernel, out_shape=jax.ShapeDtypeStruct((T, T), BF16), in_s...  88 us
    unnamed x1, local copies, waits for them, and re-layouts  1.87 us

profile of v9, /device:TPU:1, one launch (start us, length us, event | category | flops | bytes accessed | tf_op | source)
XLA Modules:
  0.0 89.9 jit_solution(17124478003294374111)
XLA Ops:
  0.0 88.0 %shard_map.109 = bf16[512,512]{1,0:T(8,128)(2,1)} custom-call(bf16[512,512]{1,0:T(8,128)(2,1)} %query_here.1, bf16[512,512]{1,0:T(8,128)(2,1)} %key_here.1, bf16[512,512]{1,0:T(8,128)(2,1)} %value_here.1, f32[1,512]{1,0:T(1,128)} %bitcast.7, bf16[8192,128]{1,0:T(8,128)(2,1)} %bitcast.6, bf16[512,4096]{1,0:T(8,128)(2,1)} %weight_here.1, ...), custom_call_target="tpu_custom_call" | custom-call | flops 12000000000 | bytes 8388608 | tf_op jit(solution)/shard_map/pallas_call | solution.py:456
  88.0 1.9 %copy.14 = bf16[512,512]{1,0:T(8,128)(2,1)} copy(bf16[512,512]{1,0:T(8,128)(2,1)} %shard_map.109) | data formatting | bytes 1048576

commit v10 on v8

--- a/solution.py
+++ b/solution.py
@@ -242,16 +242,13 @@
             staging[pl.ds(i, L, stride=Q), :] = gated[:, i * L : (i + 1) * L]
         gated_out[g] = staging[...].astype(BF16).reshape(S, C, L)
 
-    def prepare_filter():
+    def prepare_filter(g):
         @pl.loop(0, KL)
         def _(k):
             block = spectra[pl.ds(pl.multiple_of(k * T, T), T), :]
-            moved = dot(block, order[...], 0, 0)
-            for g in range(G):
-                wide[g, pl.ds(k, L, stride=KL), :] = moved[:, g * L : (g + 1) * L]
-
-    def round_filter(g):
-        filter_out[g] = wide[g].astype(BF16).reshape(S, Q, KL, L)
+            wide[pl.ds(k, L, stride=KL), :] = dot(block, order[:, chunk_lanes(g)], 0, 0)
+
+        filter_out[g] = wide[...].astype(BF16).reshape(S, Q, KL, L)
 
     def transform(g):
         staging[...] = gated_in[g].reshape(T, L).astype(F32)
@@ -371,23 +368,23 @@
     for load in loads[:2]:
         load.wait()
 
-    @pl.loop(0, G)
-    def _(g):
-        prepare_gated(g)
-
+    prepare_gated(0)
     for load in loads[2:4]:
         load.wait()
-    prepare_filter()
-    round_filter(0)
+    prepare_filter(0)
     pl.semaphore_wait(barrier, S + Z - 2)
     follow(0)
-    round_filter(1)
+    prepare_gated(1)
+    prepare_filter(1)
     follow(1)
     for load in loads[4:]:
         load.wait()
     spread_share()
-    round_filter(2)
-    round_filter(3)
+
+    @pl.loop(2, G)
+    def _(g):
+        prepare_gated(g)
+        prepare_filter(g)
 
     begin(0)
     convolve(0)
@@ -465,7 +462,7 @@
             VMEM((C, Z * T), BF16),
             VMEM((Z, S, C, T), BF16),
             VMEM((T, Z * T), BF16),
-            VMEM((G, L * KL, L), F32),
+            VMEM((L * KL, L), F32),
             VMEM((T, 2 * T), BF16),
             VMEM((G, K, T), F32),
             VMEM((K, T), BF16),

time: 86.5 us -> 90.3 us (1.044)
  Pallas kernels: 84.5 us -> 88.3 us
    pallas_call x1, Pallas kernels: 84.5 us -> 88.3 us  [body(): pl.pallas_call(kernel, out_shape=jax.ShapeDtypeStruct((T, T), BF16), in_s...]
where the time goes in v10:
time: 90.3 us; the launch traced here: 90.2 us
  Pallas kernels  88.3 us (98%)
  local copies, waits for them, and re-layouts  1.87 us (2%)
    pallas_call x1, Pallas kernels, body(): pl.pallas_call(kernel, out_shape=jax.ShapeDtypeStruct((T, T), BF16), in_s...  88.3 us
    unnamed x1, local copies, waits for them, and re-layouts  1.87 us

profile of v10, /device:TPU:1, one launch (start us, length us, event | category | flops | bytes accessed | tf_op | source)
XLA Modules:
  0.0 90.2 jit_solution(10730448642337213476)
XLA Ops:
  0.0 88.3 %shard_map.109 = bf16[512,512]{1,0:T(8,128)(2,1)} custom-call(bf16[512,512]{1,0:T(8,128)(2,1)} %query_here.1, bf16[512,512]{1,0:T(8,128)(2,1)} %key_here.1, bf16[512,512]{1,0:T(8,128)(2,1)} %value_here.1, f32[1,512]{1,0:T(1,128)} %bitcast.7, bf16[8192,128]{1,0:T(8,128)(2,1)} %bitcast.6, bf16[512,4096]{1,0:T(8,128)(2,1)} %weight_here.1, ...), custom_call_target="tpu_custom_call" | custom-call | flops 12000000000 | bytes 8388608 | tf_op jit(solution)/shard_map/pallas_call | solution.py:440
  88.3 1.9 %copy.14 = bf16[512,512]{1,0:T(8,128)(2,1)} copy(bf16[512,512]{1,0:T(8,128)(2,1)} %shard_map.109) | data formatting | bytes 1048576

commit v11 on v8

--- a/solution.py
+++ b/solution.py
@@ -396,22 +396,22 @@
     combine(0)
     convolve(1)
     follow(3)
+    forward(2, 0)
     begin(2)
-    forward(2, 0)
     combine(1)
+    forward(3, 0)
     convolve(2)
     weight_first()
-    forward(3, 0)
     begin(3)
     forward(2, 1)
     convolve(3)
     combine(2)
+    forward(4, 0)
     forward(3, 1)
     weight_second()
-    forward(4, 0)
     combine(3)
+    forward(2, 2)
     forward(4, 1)
-    forward(2, 2)
     forward(2, 3)
     forward(3, 2)
     weight_third()

time: 86.5 us -> 87 us (level)
  no operation moved by 1% of the time
where the time goes in v11:
time: 87 us; the launch traced here: 86.9 us
  Pallas kernels  85 us (98%)
  local copies, waits for them, and re-layouts  1.87 us (2%)
    pallas_call x1, Pallas kernels, body(): pl.pallas_call(kernel, out_shape=jax.ShapeDtypeStruct((T, T), BF16), in_s...  85 us
    unnamed x1, local copies, waits for them, and re-layouts  1.87 us

profile of v11, /device:TPU:1, one launch (start us, length us, event | category | flops | bytes accessed | tf_op | source)
XLA Modules:
  0.0 86.9 jit_solution(5920453021184470122)
XLA Ops:
  0.0 85.0 %shard_map.109 = bf16[512,512]{1,0:T(8,128)(2,1)} custom-call(bf16[512,512]{1,0:T(8,128)(2,1)} %query_here.1, bf16[512,512]{1,0:T(8,128)(2,1)} %key_here.1, bf16[512,512]{1,0:T(8,128)(2,1)} %value_here.1, f32[1,512]{1,0:T(1,128)} %bitcast.7, bf16[8192,128]{1,0:T(8,128)(2,1)} %bitcast.6, bf16[512,4096]{1,0:T(8,128)(2,1)} %weight_here.1, ...), custom_call_target="tpu_custom_call" | custom-call | flops 12000000000 | bytes 8388608 | tf_op jit(solution)/shard_map/pallas_call | solution.py:443
  85.0 1.9 %copy.14 = bf16[512,512]{1,0:T(8,128)(2,1)} copy(bf16[512,512]{1,0:T(8,128)(2,1)} %shard_map.109) | data formatting | bytes 1048576
